TPU v7x, 32 devices: a whole 2x2x4 slice. The times are simulated.
32 devices in a mesh: wide: 4 (over z), narrow: 8 (over y, x, core).
Axes of the slice: x: 2, y: 2, z: 4, core: 2. Of those that a mesh axis runs over, the one named last changes fastest.
Arguments:
- tokens: bfloat16 [64, 1024, 512], P(('wide', 'narrow')), may hold values from -6 to 6
- cotangent: bfloat16 [64, 1024, 512], P(('wide', 'narrow')), may hold values from -6 to 6
- seq_counts: int32 [32], replicated, may hold values from 1 to 2, as said below
- micro_assign: int32 [32, 2], replicated, may hold values from 0 to 1, each once within a row
- norm_params: float32 [4, 512], P(None, ('wide', 'narrow'))
- norm_first: float32 [4, 512], P(None, ('wide', 'narrow'))
- norm_second: float32 [4, 512], P(None, ('wide', 'narrow'))
- project_weight: float32 [512, 1536], P(('wide', 'narrow')), may hold values from -0.25 to 0.25
- project_first: float32 [512, 1536], P(('wide', 'narrow'))
- project_second: float32 [512, 1536], P(('wide', 'narrow'))
- output_weight: float32 [512, 512], P(('wide', 'narrow')), may hold values from -2 to 2
- output_first: float32 [512, 512], P(('wide', 'narrow'))
- output_second: float32 [512, 512], P(('wide', 'narrow'))
- control_weight: float32 [512, 8], P(('wide', 'narrow')), may hold values from -0.125 to 0.125
- control_first: float32 [512, 8], P(('wide', 'narrow'))
- control_second: float32 [512, 8], P(('wide', 'narrow'))
- up_weight: float32 [8, 512, 2048], P('narrow', 'wide'), may hold values from -1 to 1
- up_first: float32 [8, 512, 2048], P('narrow', 'wide')
- up_second: float32 [8, 512, 2048], P('narrow', 'wide')
- down_weight: float32 [8, 2048, 512], P('narrow', 'wide'), may hold values from -1 to 1
- down_first: float32 [8, 2048, 512], P('narrow', 'wide')
- down_second: float32 [8, 2048, 512], P('narrow', 'wide')
Outputs:
- out_rows: bfloat16 [64, 1024, 512], P(('wide', 'narrow'))
- grad_tokens: float32 [64, 1024, 512], P(('wide', 'narrow'))
- grad_norm: float32 [], replicated
- norm_new: float32 [4, 512], P(None, ('wide', 'narrow'))
- norm_first_new: float32 [4, 512], P(None, ('wide', 'narrow'))
- norm_second_new: float32 [4, 512], P(None, ('wide', 'narrow'))
- norm_low: bfloat16 [4, 512], P(None, ('wide', 'narrow'))
- project_new: float32 [512, 1536], P(('wide', 'narrow'))
- project_first_new: float32 [512, 1536], P(('wide', 'narrow'))
- project_second_new: float32 [512, 1536], P(('wide', 'narrow'))
- project_low: bfloat16 [512, 1536], P(('wide', 'narrow'))
- output_new: float32 [512, 512], P(('wide', 'narrow'))
- output_first_new: float32 [512, 512], P(('wide', 'narrow'))
- output_second_new: float32 [512, 512], P(('wide', 'narrow'))
- output_low: bfloat16 [512, 512], P(('wide', 'narrow'))
- control_new: float32 [512, 8], P(('wide', 'narrow'))
- control_first_new: float32 [512, 8], P(('wide', 'narrow'))
- control_second_new: float32 [512, 8], P(('wide', 'narrow'))
- control_low: bfloat16 [512, 8], P(('wide', 'narrow'))
- up_new: float32 [8, 512, 2048], P('narrow', 'wide')
- up_first_new: float32 [8, 512, 2048], P('narrow', 'wide')
- up_second_new: float32 [8, 512, 2048], P('narrow', 'wide')
- up_low: bfloat16 [8, 512, 2048], P('narrow', 'wide')
- down_new: float32 [8, 2048, 512], P('narrow', 'wide')
- down_first_new: float32 [8, 2048, 512], P('narrow', 'wide')
- down_second_new: float32 [8, 2048, 512], P('narrow', 'wide')
- down_low: bfloat16 [8, 2048, 512], P('narrow', 'wide')
Inputs may be any that keep to these rules, and one draw needn't show every extreme that they name: `seq_counts`: among the devices that share an index of wide, at least one holds 2 live slots; live slots are the first ones of a device. `micro_assign`: each row names every micro-batch once.
All inputs are finite; a program needn't handle non-finite values.
Results may differ from a plain program's by a relative error of at most 0.019.
Values may be sent and summed in bfloat16 or wider, within the bound.
A program may use at most 320 MiB of HBM per device.

v0:
```python
import math

import jax
import jax.numpy as jnp
from jax import lax
from jax.sharding import PartitionSpec as P

HEADS = 8
STEP = 5


PRECISE = lax.Precision.HIGHEST
NEG_LARGE = -1e30
NORM_EPS = 1e-05
CLIP_NORM = 0.05
BETA_ONE = 0.5
BETA_TWO = 0.5
ADAM_EPS = 1e-08
DECAY_RATE = 0.1


def layer_norm(values, norm_gain, norm_bias):
    row_mean = jnp.mean(values, axis=-1, keepdims=True)
    centred = values - row_mean
    variance = jnp.mean(centred * centred, axis=-1, keepdims=True)
    return centred * lax.rsqrt(variance + NORM_EPS) * norm_gain + norm_bias


def block_scores(query_block, key_heads, row_start, row_stop, scaling):
    scores = (
        jnp.einsum(
            "qhd,khd->hqk", query_block, key_heads[:row_stop], preferred_element_type=jnp.float32
        )
        * scaling
    )
    causal = jnp.arange(row_stop)[None, :] <= jnp.arange(row_start, row_stop)[:, None]
    return jnp.where(causal[None], scores, NEG_LARGE)


def attend(queries, key_rows, values, head_count):
    length, model_width = queries.shape
    head_size = model_width // head_count
    block_rows = min(512, length)
    scaling = 1.0 / math.sqrt(head_size)
    query_heads = queries.reshape(length, head_count, head_size)
    key_heads = key_rows.reshape(length, head_count, head_size)
    value_heads = values.reshape(length, head_count, head_size)
    outputs = []
    log_sums = []
    for row_start in range(0, length, block_rows):
        row_stop = row_start + block_rows
        scores = block_scores(
            query_heads[row_start:row_stop], key_heads, row_start, row_stop, scaling
        )
        row_max = jnp.max(scores, axis=-1, keepdims=True)
        exponent = jnp.exp(scores - row_max)
        row_total = jnp.sum(exponent, axis=-1, keepdims=True)
        probs_low = (exponent / row_total).astype(jnp.bfloat16)
        block_out = jnp.einsum(
            "hqk,khd->qhd", probs_low, value_heads[:row_stop], preferred_element_type=jnp.float32
        )
        outputs.append(block_out.reshape(block_rows, model_width))
        log_sums.append(row_max + jnp.log(row_total))
    return (jnp.concatenate(outputs, axis=0).astype(jnp.bfloat16), log_sums)


def attend_back(queries, key_rows, values, grad_attended, log_sums, head_count):
    length, model_width = queries.shape
    head_size = model_width // head_count
    block_rows = min(512, length)
    scaling = 1.0 / math.sqrt(head_size)
    query_heads = queries.reshape(length, head_count, head_size)
    key_heads = key_rows.reshape(length, head_count, head_size)
    value_heads = values.reshape(length, head_count, head_size)
    grad_heads = grad_attended.reshape(length, head_count, head_size)
    grad_query = []
    grad_key = jnp.zeros((length, head_count, head_size), jnp.float32)
    grad_value = jnp.zeros((length, head_count, head_size), jnp.float32)
    for block_index, row_start in enumerate(range(0, length, block_rows)):
        row_stop = row_start + block_rows
        query_block = query_heads[row_start:row_stop]
        scores = block_scores(query_block, key_heads, row_start, row_stop, scaling)
        probs = jnp.exp(scores - log_sums[block_index])
        probs_low = probs.astype(jnp.bfloat16)
        grad_block = grad_heads[row_start:row_stop]
        grad_value = grad_value.at[:row_stop].add(
            jnp.einsum("hqk,qhd->khd", probs_low, grad_block, preferred_element_type=jnp.float32)
        )
        grad_probs = jnp.einsum(
            "qhd,khd->hqk", grad_block, value_heads[:row_stop], preferred_element_type=jnp.float32
        )
        inner = jnp.sum(probs * grad_probs, axis=-1, keepdims=True)
        grad_scores = (probs * (grad_probs - inner)).astype(jnp.bfloat16)
        grad_query.append(
            jnp.einsum(
                "hqk,khd->qhd",
                grad_scores,
                key_heads[:row_stop],
                preferred_element_type=jnp.float32,
            )
            * scaling
        )
        grad_key = grad_key.at[:row_stop].add(
            jnp.einsum("hqk,qhd->khd", grad_scores, query_block, preferred_element_type=jnp.float32)
            * scaling
        )
    grad_project = jnp.concatenate(
        [
            jnp.concatenate(grad_query, axis=0).reshape(length, model_width),
            grad_key.reshape(length, model_width),
            grad_value.reshape(length, model_width),
        ],
        axis=1,
    )
    return grad_project.astype(jnp.bfloat16)


def adam_update(weight, first_state, second_state, gradient, factor, rate, decay):
    clipped = gradient * factor
    first_new = BETA_ONE * first_state + (1.0 - BETA_ONE) * clipped
    second_new = BETA_TWO * second_state + (1.0 - BETA_TWO) * clipped * clipped
    first_hat = first_new / (1.0 - BETA_ONE**STEP)
    second_hat = second_new / (1.0 - BETA_TWO**STEP)
    weight_new = weight - rate * (first_hat / (jnp.sqrt(second_hat) + ADAM_EPS) + decay * weight)
    return (weight_new, first_new, second_new, weight_new.astype(jnp.bfloat16))


def per_device(
    tokens,
    cotangent,
    seq_counts,
    micro_assign,
    norm_params,
    norm_first,
    norm_second,
    project_weight,
    project_first,
    project_second,
    output_weight,
    output_first,
    output_second,
    control_weight,
    control_first,
    control_second,
    up_weight,
    up_first,
    up_second,
    down_weight,
    down_first,
    down_second,
):
    norm_all, project_all, output_all, control_all = (
        lax.all_gather(norm_params, ("wide", "narrow"), axis=1, tiled=True),
        lax.all_gather(project_weight, ("wide", "narrow"), axis=0, tiled=True),
        lax.all_gather(output_weight, ("wide", "narrow"), axis=0, tiled=True),
        lax.all_gather(control_weight, ("wide", "narrow"), axis=0, tiled=True),
    )
    up_all, down_all = (
        lax.all_gather(up_weight.astype(jnp.bfloat16), "wide", axis=1, tiled=True),
        lax.all_gather(down_weight.astype(jnp.bfloat16), "wide", axis=1, tiled=True),
    )
    project_low = project_all.astype(jnp.bfloat16)
    output_low = output_all.astype(jnp.bfloat16)
    control_low = control_all.astype(jnp.bfloat16)
    member_count = lax.axis_size("narrow")
    narrow_index = lax.axis_index("narrow")
    wide_index = lax.axis_index("wide")
    micro_count, length, model_width = tokens.shape
    owned_experts = up_weight.shape[0]
    first_device = wide_index * member_count
    row_counts = lax.dynamic_slice_in_dim(seq_counts, first_device, member_count)
    row_assign = lax.dynamic_slice_in_dim(micro_assign, first_device, member_count, 0)
    slot_numbers = jnp.arange(micro_count, dtype=jnp.int32)
    grad_norms = jnp.zeros(norm_all.shape, jnp.float32)
    grad_project_w = jnp.zeros(project_all.shape, jnp.float32)
    grad_output_w = jnp.zeros(output_all.shape, jnp.float32)
    grad_control_w = jnp.zeros(control_all.shape, jnp.float32)
    grad_up_w = jnp.zeros(up_all.shape, jnp.float32)
    grad_down_w = jnp.zeros(down_all.shape, jnp.float32)
    grad_tokens = jnp.zeros(tokens.shape, jnp.float32)
    out_rows = jnp.zeros(tokens.shape, jnp.bfloat16)
    for micro_batch in range(micro_count):
        member_slots = jnp.sum(
            slot_numbers[None, :] * (row_assign == micro_batch).astype(jnp.int32), axis=1
        )
        live_member = (member_slots < row_counts).astype(jnp.float32)
        own_slot = lax.dynamic_index_in_dim(member_slots, narrow_index, 0, keepdims=False)
        inputs = lax.dynamic_index_in_dim(tokens, own_slot, 0, keepdims=False)
        target = lax.dynamic_index_in_dim(cotangent, own_slot, 0, keepdims=False)
        target_full = target.astype(jnp.float32)
        residual = inputs.astype(jnp.float32)
        normed_one = layer_norm(residual, norm_all[0], norm_all[1]).astype(jnp.bfloat16)
        project = jnp.dot(normed_one, project_low, preferred_element_type=jnp.float32).astype(
            jnp.bfloat16
        )
        queries = project[:, :model_width]
        key_rows = project[:, model_width : 2 * model_width]
        values = project[:, 2 * model_width :]
        attended, log_sums = attend(queries, key_rows, values, HEADS)
        hidden = residual + jnp.dot(attended, output_low, preferred_element_type=jnp.float32)
        normed_two = layer_norm(hidden, norm_all[2], norm_all[3]).astype(jnp.bfloat16)
        logits = jnp.dot(normed_two, control_low, preferred_element_type=jnp.float32).astype(
            jnp.bfloat16
        )
        group_in, group_target, group_logits = (
            lax.all_gather(normed_two[None], "narrow", axis=0, tiled=True),
            lax.all_gather(target[None], "narrow", axis=0, tiled=True),
            lax.all_gather(logits[None], "narrow", axis=0, tiled=True),
        )
        live_cube = live_member[:, None, None]
        masked = jnp.where(live_cube > 0, group_logits.astype(jnp.float32), NEG_LARGE)
        col_max = jnp.max(masked, axis=0, keepdims=True)
        exponent = jnp.exp(masked - col_max) * live_cube
        weights = exponent / jnp.sum(exponent, axis=0, keepdims=True)
        own_weights = lax.dynamic_index_in_dim(weights, narrow_index, 0, keepdims=False)
        normed_full = normed_two.astype(jnp.float32)
        owned_weights = lax.dynamic_slice_in_dim(
            weights, narrow_index * owned_experts, owned_experts, 2
        )
        mixture_pre = jnp.einsum(
            "nlx,nld->xld", owned_weights, group_in.astype(jnp.float32), precision=PRECISE
        )
        back_pre = jnp.einsum(
            "nlx,nld->xld", owned_weights, group_target.astype(jnp.float32), precision=PRECISE
        )
        mixture_low = mixture_pre.astype(jnp.bfloat16)
        hidden_pre = jnp.einsum(
            "xld,xdf->xlf", mixture_low, up_all, preferred_element_type=jnp.float32
        )
        hidden_act = jax.nn.gelu(hidden_pre).astype(jnp.bfloat16)
        expert_out = jnp.einsum(
            "xlf,xfd->xld", hidden_act, down_all, preferred_element_type=jnp.float32
        ).astype(jnp.bfloat16)
        back_low = back_pre.astype(jnp.bfloat16)
        grad_down_w = grad_down_w + jnp.einsum(
            "xlf,xld->xfd", hidden_act, back_low, preferred_element_type=jnp.float32
        )
        grad_act = jnp.einsum(
            "xld,xfd->xlf", back_low, down_all, preferred_element_type=jnp.float32
        )
        grad_pre = jax.vjp(jax.nn.gelu, hidden_pre)[1](grad_act)[0].astype(jnp.bfloat16)
        grad_up_w = grad_up_w + jnp.einsum(
            "xld,xlf->xdf", mixture_low, grad_pre, preferred_element_type=jnp.float32
        )
        grad_mixture = jnp.einsum(
            "xlf,xdf->xld", grad_pre, up_all, preferred_element_type=jnp.float32
        ).astype(jnp.bfloat16)
        piece_full = lax.all_gather(expert_out, "narrow", axis=0, tiled=True).astype(jnp.float32)
        mixed_sum = jnp.einsum("lx,xld->ld", own_weights, piece_full, precision=PRECISE)
        paired = jnp.einsum("ld,xld->lx", target_full, piece_full, precision=PRECISE)
        out_rows = lax.dynamic_update_index_in_dim(
            out_rows, (hidden + mixed_sum).astype(jnp.bfloat16), own_slot, 0
        )
        spread_piece_full = lax.all_gather(grad_mixture, "narrow", axis=0, tiled=True).astype(
            jnp.float32
        )
        grad_sum = jnp.einsum("lx,xld->ld", own_weights, spread_piece_full, precision=PRECISE)
        spread_paired = jnp.einsum("ld,xld->lx", normed_full, spread_piece_full, precision=PRECISE)
        grad_normed_two = grad_sum
        grad_weights = spread_paired + paired
        group_sum = lax.psum(own_weights * grad_weights, "narrow")
        grad_logits = (own_weights * (grad_weights - group_sum)).astype(jnp.bfloat16)
        grad_control_w = grad_control_w + jnp.einsum(
            "ld,le->de", normed_two, grad_logits, preferred_element_type=jnp.float32
        )
        grad_normed_two = grad_normed_two + jnp.einsum(
            "le,de->ld", grad_logits, control_low, preferred_element_type=jnp.float32
        )
        norm_back_two = jax.vjp(layer_norm, hidden, norm_all[2], norm_all[3])[1]
        grad_hidden, grad_gain_two, grad_bias_two = norm_back_two(grad_normed_two)
        grad_hidden = grad_hidden + target_full
        grad_branch = grad_hidden.astype(jnp.bfloat16)
        grad_output_w = grad_output_w + jnp.einsum(
            "ld,le->de", attended, grad_branch, preferred_element_type=jnp.float32
        )
        grad_attended = jnp.einsum(
            "le,de->ld", grad_branch, output_low, preferred_element_type=jnp.float32
        ).astype(jnp.bfloat16)
        grad_project = attend_back(queries, key_rows, values, grad_attended, log_sums, HEADS)
        grad_project_w = grad_project_w + jnp.einsum(
            "ld,le->de", normed_one, grad_project, preferred_element_type=jnp.float32
        )
        grad_normed_one = jnp.einsum(
            "le,de->ld", grad_project, project_low, preferred_element_type=jnp.float32
        )
        norm_back_one = jax.vjp(layer_norm, residual, norm_all[0], norm_all[1])[1]
        grad_residual, grad_gain_one, grad_bias_one = norm_back_one(grad_normed_one)
        grad_norms = grad_norms + jnp.stack(
            [grad_gain_one, grad_bias_one, grad_gain_two, grad_bias_two]
        )
        grad_tokens = lax.dynamic_update_index_in_dim(
            grad_tokens, grad_hidden + grad_residual, own_slot, 0
        )
    up_grad, down_grad = (
        lax.psum_scatter(grad_up_w, "wide", scatter_dimension=1, tiled=True),
        lax.psum_scatter(grad_down_w, "wide", scatter_dimension=1, tiled=True),
    )
    norm_grad, project_grad, output_grad, control_grad = (
        lax.psum_scatter(grad_norms, ("wide", "narrow"), scatter_dimension=1, tiled=True),
        lax.psum_scatter(grad_project_w, ("wide", "narrow"), scatter_dimension=0, tiled=True),
        lax.psum_scatter(grad_output_w, ("wide", "narrow"), scatter_dimension=0, tiled=True),
        lax.psum_scatter(grad_control_w, ("wide", "narrow"), scatter_dimension=0, tiled=True),
    )
    squares = jnp.float32(0.0)
    for gradient in (norm_grad, project_grad, output_grad, control_grad, up_grad, down_grad):
        squares = squares + jnp.sum(gradient * gradient)
    grad_norm = jnp.sqrt(lax.psum(squares, ("wide", "narrow")))
    factor = CLIP_NORM / jnp.maximum(grad_norm, CLIP_NORM)
    norm_out = adam_update(norm_params, norm_first, norm_second, norm_grad, factor, 0.3, 0.0)
    project_out = adam_update(
        project_weight, project_first, project_second, project_grad, factor, 0.03, DECAY_RATE
    )
    output_out = adam_update(
        output_weight, output_first, output_second, output_grad, factor, 0.2, DECAY_RATE
    )
    control_out = adam_update(
        control_weight, control_first, control_second, control_grad, factor, 0.015, DECAY_RATE
    )
    up_out = adam_update(up_weight, up_first, up_second, up_grad, factor, 0.1, DECAY_RATE)
    down_out = adam_update(down_weight, down_first, down_second, down_grad, factor, 0.1, DECAY_RATE)
    return (
        out_rows,
        grad_tokens,
        grad_norm,
        norm_out[0],
        norm_out[1],
        norm_out[2],
        norm_out[3],
        project_out[0],
        project_out[1],
        project_out[2],
        project_out[3],
        output_out[0],
        output_out[1],
        output_out[2],
        output_out[3],
        control_out[0],
        control_out[1],
        control_out[2],
        control_out[3],
        up_out[0],
        up_out[1],
        up_out[2],
        up_out[3],
        down_out[0],
        down_out[1],
        down_out[2],
        down_out[3],
    )


def solution(mesh):
    return jax.shard_map(
        per_device,
        mesh=mesh,
        in_specs=(
            P(("wide", "narrow"), None, None),
            P(("wide", "narrow"), None, None),
            P(),
            P(),
            P(None, ("wide", "narrow")),
            P(None, ("wide", "narrow")),
            P(None, ("wide", "narrow")),
            P(("wide", "narrow"), None),
            P(("wide", "narrow"), None),
            P(("wide", "narrow"), None),
            P(("wide", "narrow"), None),
            P(("wide", "narrow"), None),
            P(("wide", "narrow"), None),
            P(("wide", "narrow"), None),
            P(("wide", "narrow"), None),
            P(("wide", "narrow"), None),
            P("narrow", "wide", None),
            P("narrow", "wide", None),
            P("narrow", "wide", None),
            P("narrow", "wide", None),
            P("narrow", "wide", None),
            P("narrow", "wide", None),
        ),
        out_specs=(
            P(("wide", "narrow"), None, None),
            P(("wide", "narrow"), None, None),
            P(),
            P(None, ("wide", "narrow")),
            P(None, ("wide", "narrow")),
            P(None, ("wide", "narrow")),
            P(None, ("wide", "narrow")),
            P(("wide", "narrow"), None),
            P(("wide", "narrow"), None),
            P(("wide", "narrow"), None),
            P(("wide", "narrow"), None),
            P(("wide", "narrow"), None),
            P(("wide", "narrow"), None),
            P(("wide", "narrow"), None),
            P(("wide", "narrow"), None),
            P(("wide", "narrow"), None),
            P(("wide", "narrow"), None),
            P(("wide", "narrow"), None),
            P(("wide", "narrow"), None),
            P("narrow", "wide", None),
            P("narrow", "wide", None),
            P("narrow", "wide", None),
            P("narrow", "wide", None),
            P("narrow", "wide", None),
            P("narrow", "wide", None),
            P("narrow", "wide", None),
            P("narrow", "wide", None),
        ),
        check_vma=False,
    )
```

profile of v0, /device:TPU:0, one launch (start us, length us, event | category | flops | bytes accessed | tf_op | source)
XLA Modules:
  0.0 1463.1 jit_solution(1420805675990175169)
XLA Ops:
  21.2 43.5 %all-gather.8 = f32[32,16,4]{1,2,0:T(4,128)S(1)} all-gather(f32[1,16,4]{1,2,0:T(4,128)S(1)} %bitcast.454), channel_id=1, replica_groups=mesh['wide'=4,'narrow'=8] {'wide','narrow'}, dimensions={0}, use_global_device_ids=true | all-gather | bytes 8448 | tf_op jit(solution)/shard_map/all_gather | solution.py:153
  66.1 41.1 %all_gather.50 = bf16[512,512]{1,0:T(8,128)(2,1)} all-gather(bf16[16,512]{1,0:T(8,128)(2,1)S(1)} %convert.150), channel_id=1, replica_groups=mesh['wide'=4,'narrow'=8] {'wide','narrow'}, dimensions={0}, use_global_device_ids=true | all-gather | bytes 540672 | tf_op jit(solution)/shard_map/all_gather | solution.py:155
  193.6 39.2 %all-gather.9 = bf16[32,16,8]{1,2,0:T(8,128)(2,1)S(1)} all-gather(bf16[1,16,8]{1,2,0:T(8,128)(2,1)S(1)} %bitcast_convert_fusion.8), channel_id=1, replica_groups=mesh['wide'=4,'narrow'=8] {'wide','narrow'}, dimensions={0}, use_global_device_ids=true | all-gather | bytes 8448 | tf_op jit(solution)/shard_map/all_gather | solution.py:156
  242.5 15.2 %fusion.24 = bf16[1024,1,512]{2,1,0:T(2,128)(2,1)} fusion(f32[8,1024,1]{0,2,1:T(1,128)S(1)} %bitcast.430, bf16[8,1024,512]{2,1,0:T(8,128)(2,1)} %all-gather.28.cloned.1.call-done), kind=kOutput, calls=%fused_computation.48 | convolution fusion | flops 50331648 | bytes 9469952 | tf_op jit(solution)/shard_map/nlx,nld->xld/dot_general | solution.py:223
  257.8 16.4 %copy.298 = bf16[64,8,8,1024]{3,2,1,0:T(8,128)(2,1)} copy(bf16[64,8,8,1024]{3,1,2,0:T(8,128)(2,1)} %bitcast.382) | data formatting | bytes 16777216
  298.5 39.4 %all-gather.26.cloned.1.call-done = bf16[1,2048,512]{2,1,0:T(8,128)(2,1)} async-done(((bf16[1,512,512]{2,1,0:T(8,128)(2,1)}), bf16[1,2048,512]{2,1,0:T(8,128)(2,1)}) %all-gather.26.cloned.1.call-update) | async-done | bytes 2097168 | tf_op jit(solution)/shard_map/all_gather | solution.py:160
  337.9 10.4 fusion.10
  364.5 29.4 %all-gather.30.cloned.1.call-done = bf16[8,1024,512]{2,1,0:T(8,128)(2,1)} async-done(((bf16[1,1024,512]{2,1,0:T(8,128)(2,1)}), bf16[8,1024,512]{2,1,0:T(8,128)(2,1)}) %all-gather.30.cloned.1.call-update) | async-done | bytes 8388624 | tf_op jit(solution)/shard_map/all_gather | solution.py:207
  393.9 15.2 %fusion.22 = bf16[1024,1,512]{2,1,0:T(2,128)(2,1)} fusion(f32[8,1024,1]{0,2,1:T(1,128)S(1)} %bitcast.431, bf16[8,1024,512]{2,1,0:T(8,128)(2,1)} %all-gather.30.cloned.1.call-done), kind=kOutput, calls=%fused_computation.46 | convolution fusion | flops 50331648 | bytes 9469952 | tf_op jit(solution)/shard_map/nlx,nld->xld/dot_general | solution.py:223
  409.1 41.7 %all-gather.36.cloned.1.call-done = bf16[8192,512]{0,1:T(8,128)(2,1)} async-done(((bf16[1024,512]{0,1:T(8,128)(2,1)}), bf16[8192,512]{0,1:T(8,128)(2,1)}) %all-gather.36.cloned.1.call-update) | async-done | bytes 8388624 | tf_op jit(solution)/shard_map/all_gather | solution.py:206
  450.8 16.4 %copy.299 = bf16[64,8,8,1024]{3,2,1,0:T(8,128)(2,1)} copy(bf16[64,8,8,1024]{3,1,2,0:T(8,128)(2,1)} %bitcast.381) | data formatting | bytes 16777216
  467.2 10.5 multiply_reduce_fusion.7
  546.5 16.9 %all-gather.42.cloned.1.call-done = bf16[8192,512]{1,0:T(8,128)(2,1)} async-done(((bf16[1024,512]{1,0:T(8,128)(2,1)}), bf16[8192,512]{1,0:T(8,128)(2,1)}) %all-gather.42.cloned.1.call-update) | async-done | bytes 8388624 | tf_op jit(solution)/shard_map/all_gather | solution.py:254
  568.5 51.0 %all-gather.38.cloned.1.call-done = bf16[8192,512]{1,0:T(8,128)(2,1)} async-done(((bf16[1024,512]{1,0:T(8,128)(2,1)}), bf16[8192,512]{1,0:T(8,128)(2,1)}) %all-gather.38.cloned.1.call-update) | async-done | bytes 8388624 | tf_op jit(solution)/shard_map/all_gather | solution.py:248
  626.0 49.8 %all-gather.34.cloned.1.call-done = bf16[8192,512]{1,0:T(8,128)(2,1)} async-done(((bf16[1024,512]{1,0:T(8,128)(2,1)}), bf16[8192,512]{1,0:T(8,128)(2,1)}) %all-gather.34.cloned.1.call-update) | async-done | bytes 8388624 | tf_op jit(solution)/shard_map/all_gather | solution.py:248
  682.7 11.3 add_bitcast_fusion
  717.4 10.1 multiply_reduce_fusion.5
  779.4 10.3 multiply_convert_fusion.1
  840.8 12.2 multiply_convert_fusion
  933.7 96.3 %reduce-scatter.19.cloned.1.call-done = f32[16,4]{1,0:T(8,128)} async-done(((f32[512,4]{1,0:T(8,128)}), f32[16,4]{1,0:T(8,128)}) %reduce-scatter.19.cloned.1.call-update) | async-done | bytes 272
  1031.4 130.6 %reduce-scatter.21.cloned.1.call-done = f32[16,8]{1,0:T(8,128)} async-done(((f32[512,8]{1,0:T(8,128)}), f32[16,8]{1,0:T(8,128)}) %reduce-scatter.21.cloned.1.call-update) | async-done | bytes 528
  1163.4 132.1 %reduce-scatter.13.cloned.1.call-done = f32[16,512]{1,0:T(8,128)} async-done(((f32[512,512]{1,0:T(8,128)}), f32[16,512]{1,0:T(8,128)}) %reduce-scatter.13.cloned.1.call-update) | async-done | bytes 32784 | tf_op jit(solution)/shard_map/reduce_scatter | solution.py:301
  1296.9 101.4 %reduce-scatter.11.cloned.1.call-done = f32[16,1536]{1,0:T(8,128)} async-done(((f32[512,1536]{1,0:T(8,128)}), f32[16,1536]{1,0:T(8,128)}) %reduce-scatter.11.cloned.1.call-update) | async-done | bytes 98320 | tf_op jit(solution)/shard_map/reduce_scatter | solution.py:300
  1404.8 39.8 %psum.23 = f32[]{:T(128)} all-reduce(f32[]{:T(128)S(6)} %add.477), channel_id=1, replica_groups=mesh['wide'=4,'narrow'=8] {'wide','narrow'}, use_global_device_ids=true, to_apply=%region_56.57 | all-reduce | flops 1 | bytes 8 | tf_op jit(solution)/shard_map/psum | solution.py:307
  (651 shorter events, 455.6 us)
Async XLA Ops:
  7.2 101.0 %all-gather.22.cloned.1.call-start = ((), (), s32[]{:S(2)}) async-start(), calls=%async_computation.6 | async-start | bytes 1622016 | tf_op jit(solution)/shard_map/all_gather | solution.py:154
  8.8 233.7 %all-gather.28.cloned.1.call-start = ((), (), s32[]{:S(2)}) async-start(), calls=%async_computation.9 | async-start | bytes 9437184 | tf_op jit(solution)/shard_map/all_gather | solution.py:207
  17.7 240.0 %all-gather.32.cloned.1.call-start = ((), (), s32[]{:S(2)}) async-start(), calls=%async_computation.15 | async-start | bytes 9437184 | tf_op jit(solution)/shard_map/all_gather | solution.py:206
  190.1 101.2 %all-gather.24.cloned.1.call-start = ((), (), s32[]{:S(2)}) async-start(), calls=%async_computation.7 | async-start | bytes 2621440 | tf_op jit(solution)/shard_map/all_gather | solution.py:159
  191.2 146.7 %all-gather.26.cloned.1.call-start = ((), (), s32[]{:S(2)}) async-start(), calls=%async_computation.8 | async-start | bytes 2621440 | tf_op jit(solution)/shard_map/all_gather | solution.py:160
  192.2 201.7 %all-gather.30.cloned.1.call-start = ((), (), s32[]{:S(2)}) async-start(), calls=%async_computation.10 | async-start | bytes 9437184 | tf_op jit(solution)/shard_map/all_gather | solution.py:207
  192.8 258.0 %all-gather.36.cloned.1.call-start = ((), (), s32[]{:S(2)}) async-start(), calls=%async_computation.17 | async-start | bytes 9437184 | tf_op jit(solution)/shard_map/all_gather | solution.py:206
  193.5 347.1 %all-gather.40.cloned.1.call-start = ((), (), s32[]{:S(2)}) async-start(), calls=%async_computation.19 | async-start | bytes 9437184 | tf_op jit(solution)/shard_map/all_gather | solution.py:254
  353.6 209.8 %all-gather.42.cloned.1.call-start = ((), (), s32[]{:S(2)}) async-start(), calls=%async_computation.20 | async-start | bytes 9437184 | tf_op jit(solution)/shard_map/all_gather | solution.py:254
  496.7 122.9 %all-gather.38.cloned.1.call-start = ((), (), s32[]{:S(2)}) async-start(), calls=%async_computation.18 | async-start | bytes 9437184 | tf_op jit(solution)/shard_map/all_gather | solution.py:248
  504.8 171.1 %all-gather.34.cloned.1.call-start = ((), (), s32[]{:S(2)}) async-start(), calls=%async_computation.16 | async-start | bytes 9437184 | tf_op jit(solution)/shard_map/all_gather | solution.py:248
  512.7 222.7 %all-reduce.7.cloned.1.call-start = ((), (), s32[]{:S(2)}) async-start(), calls=%async_computation.23 | async-start | bytes 131072 | tf_op jit(solution)/shard_map/psum | solution.py:261
  682.5 221.1 %reduce-scatter.17.cloned.1.call-start = ((), (), s32[]{:S(2)}) async-start(), calls=%async_computation.14 | async-start | bytes 5242880 | tf_op jit(solution)/shard_map/reduce_scatter | solution.py:296
  694.1 211.7 %reduce-scatter.15.cloned.1.call-start = ((), (), s32[]{:S(2)}) async-start(), calls=%async_computation.13 | async-start | bytes 5242880 | tf_op jit(solution)/shard_map/reduce_scatter | solution.py:295
  705.0 325.0 %reduce-scatter.19.cloned.1.call-start = ((), (), s32[]{:S(2)}) async-start(), calls=%async_computation.21 | async-start | bytes 270336
  891.1 270.9 %reduce-scatter.21.cloned.1.call-start = ((), (), s32[]{:S(2)}) async-start(), calls=%async_computation.22 | async-start | bytes 270336
  892.4 403.1 %reduce-scatter.13.cloned.1.call-start = ((), (), s32[]{:S(2)}) async-start(), calls=%async_computation.12 | async-start | bytes 1081344 | tf_op jit(solution)/shard_map/reduce_scatter | solution.py:301
  896.1 502.1 %reduce-scatter.11.cloned.1.call-start = ((), (), s32[]{:S(2)}) async-start(), calls=%async_computation.11 | async-start | bytes 3244032 | tf_op jit(solution)/shard_map/reduce_scatter | solution.py:300
  932.1 513.2 %copy-start.168 = (f32[16,8]{0,1:T(8,128)S(1)}, f32[16,8]{0,1:T(8,128)}, u32[]{:S(2)}) copy-start(f32[16,8]{0,1:T(8,128)} %param.61) | copy-start | bytes 1540
  932.1 513.8 %copy-start.166 = (f32[4,16]{1,0:T(4,128)S(1)}, f32[4,16]{1,0:T(4,128)}, u32[]{:S(2)}) copy-start(f32[4,16]{1,0:T(4,128)} %param.50) | copy-start | bytes 772
  932.2 513.8 %copy-start.169 = (f32[4,16]{1,0:T(4,128)S(1)}, f32[4,16]{1,0:T(4,128)}, u32[]{:S(2)}) copy-start(f32[4,16]{1,0:T(4,128)} %param.51) | copy-start | bytes 772
  932.2 513.8 %copy-start.170 = (f32[4,16]{1,0:T(4,128)S(1)}, f32[4,16]{1,0:T(4,128)}, u32[]{:S(2)}) copy-start(f32[4,16]{1,0:T(4,128)} %param.52) | copy-start | bytes 772
  932.2 514.4 %copy-start.61 = (f32[1,512,512]{2,1,0:T(8,128)S(1)}, f32[1,512,512]{2,1,0:T(8,128)}, u32[]{:S(2)}) copy-start(f32[1,512,512]{2,1,0:T(8,128)} %param.65) | copy-start | bytes 3145732
  932.2 514.4 %copy-start.67 = (f32[1,512,512]{2,1,0:T(8,128)S(1)}, f32[1,512,512]{2,1,0:T(8,128)}, u32[]{:S(2)}) copy-start(f32[1,512,512]{2,1,0:T(8,128)} %reduce-scatter.17.cloned.1.call-done) | copy-start | bytes 3145732
  (195 other events, 3665.5 us)
Sparse Core Ops, SparseCore 0:
  11.5 57.8 all-gather.21
  71.2 55.0 all-gather.27
  190.2 53.1 all-gather.31
  245.3 45.8 all-gather.23
  293.2 44.6 all-gather.25
  340.2 53.6 all-gather.29
  396.4 54.3 all-gather.35
  452.7 54.3 all-gather.39
  509.0 54.3 all-gather.41
  565.2 54.3 all-gather.37
  621.5 54.3 all-gather.33
  682.6 52.6 all-reduce.6
  737.7 76.1 reduce-scatter.16
  816.0 77.2 reduce-scatter.14
  896.0 133.9 reduce-scatter.18
  1032.7 129.3 reduce-scatter.20
  1164.8 130.6 reduce-scatter.12
  1300.8 97.4 reduce-scatter.10
where the time goes:
time: 1470 us; the launch traced here: 1460 us
  waiting for transfers between devices  697 us (47%)
  matrix products  249 us (17%)
  blocking collectives  181 us (12%)
  other arithmetic  158 us (11%)
  local copies, waits for them, and re-layouts  149 us (10%)
  between operations  27.1 us (2%)
    unnamed x20, waiting for transfers between devices  228 us
    reduce_scatter x1, waiting for transfers between devices, per_device(): lax.psum_scatter(grad_output_w, ('wide', 'narrow'), scatter_dimension=0,...  132 us
    reduce_scatter x1, waiting for transfers between devices, per_device(): lax.psum_scatter(grad_project_w, ('wide', 'narrow'), scatter_dimension=0,...  101 us
    all_gather x2, waiting for transfers between devices, per_device(): lax.all_gather(expert_out, 'narrow', axis=0, tiled=True).astype(jnp.float32)  101 us
    unnamed x417, local copies, waits for them, and re-layouts  70.9 us
    unnamed x14, other arithmetic  45.4 us
    all_gather x1, blocking collectives, per_device(): lax.all_gather(norm_params, ('wide', 'narrow'), axis=1, tiled=True)  43.5 us
    all_gather x2, waiting for transfers between devices, per_device(): lax.all_gather(normed_two[None], 'narrow', axis=0, tiled=True)  41.7 us
  transfers between devices with their start and end apart: 18, of which 11 were waited for; matrix products, arithmetic and copies ran while one was open for 35% of the time, Pallas kernels for 0%

commit v1 on v0

v1 whole, which is shorter than its diff:
```python
import functools
import math

import jax
import jax.numpy as jnp
from jax import lax
from jax.experimental import pallas as pl
from jax.experimental.pallas import tpu as pltpu
from jax.sharding import PartitionSpec as P

HEADS = 8
STEP = 5
NEG_LARGE = -1e30
NORM_EPS = 1e-05
CLIP_NORM = 0.05
BETA_ONE = 0.5
BETA_TWO = 0.5
ADAM_EPS = 1e-08
DECAY_RATE = 0.1

BF = jnp.bfloat16
F32 = jnp.float32
MESH = pl.DeviceIdType.MESH
LANES = 128
ROWS = 256
GELU_A = math.sqrt(2.0 / math.pi)
GELU_B = 0.044715


def dot(a, b, ca, cb):
    return lax.dot_general(a, b, (((ca,), (cb,)), ((), ())), preferred_element_type=F32)


def norm_stats(v):
    centred = v - jnp.mean(v, axis=-1, keepdims=True)
    rstd = lax.rsqrt(jnp.mean(centred * centred, axis=-1, keepdims=True) + NORM_EPS)
    return centred * rstd, rstd


def norm_back(grad, gain, xhat, rstd):
    t = grad * gain
    return rstd * (t - jnp.mean(t, axis=-1, keepdims=True) - xhat * jnp.mean(t * xhat, axis=-1, keepdims=True))


def remote(src, dst, send, recv, device):
    return pltpu.make_async_remote_copy(
        src_ref=src, dst_ref=dst, send_sem=send, recv_sem=recv, device_id=device, device_id_type=MESH
    )


def greet(devices):
    barrier = pltpu.get_barrier_semaphore()
    for device in devices:
        pl.semaphore_signal(barrier, inc=1, device_id=device, device_id_type=MESH)
    pl.semaphore_wait(barrier, len(devices))


def gather_kernel(wides, narrows, shard_ref, out_ref, local_sem, z_sem, p_sem, c_sem, recv_sem):
    w, n = lax.axis_index("wide"), lax.axis_index("narrow")
    half = narrows // 2
    q, parity = n // 2, lax.rem(n, 2)
    z_peers = [lax.rem(w + k, wides) for k in range(1, wides)]
    p_peers = [lax.rem(q + k, half) * 2 + parity for k in range(1, half)]
    core = n + 1 - 2 * parity
    greet([(z, n) for z in z_peers] + [(w, p) for p in p_peers] + [(w, core)])
    own = pltpu.make_async_copy(shard_ref, out_ref.at[w, n], local_sem)
    own.start()
    sends = []

    def send(src, zw, zn, sem, device):
        copy = remote(src, out_ref.at[zw, zn], sem, recv_sem.at[zw, zn], device)
        copy.start()
        sends.append(copy)

    def arrived(zw, zn):
        remote(shard_ref, out_ref.at[zw, zn], z_sem.at[0], recv_sem.at[zw, zn], (w, n)).wait_recv()

    for k, z in enumerate(z_peers):
        send(shard_ref, w, n, z_sem.at[k], (z, n))
    for k, p in enumerate(p_peers):
        send(shard_ref, w, n, p_sem.at[0, k], (w, p))
    send(shard_ref, w, n, c_sem.at[0, 0], (w, core))
    for j in range(1, wides):
        zw = lax.rem(w + wides - j, wides)
        arrived(zw, n)
        for k, p in enumerate(p_peers):
            send(out_ref.at[zw, n], zw, n, p_sem.at[j, k], (w, p))
        send(out_ref.at[zw, n], zw, n, c_sem.at[j, 0], (w, core))
    for i in range(1, half):
        zn = lax.rem(q + half - i, half) * 2 + parity
        for j in range(wides):
            zw = lax.rem(w + wides - j, wides)
            arrived(zw, zn)
            send(out_ref.at[zw, zn], zw, zn, c_sem.at[j, i], (w, core))
    for i in range(half):
        for j in range(wides):
            arrived(j, 2 * i + 1 - parity)
    own.wait()
    for copy in sends:
        copy.wait_send()


def gather_shared(shard, wides, narrows):
    half = narrows // 2
    hbm = pl.BlockSpec(memory_space=pl.ANY)
    return pl.pallas_call(
        functools.partial(gather_kernel, wides, narrows),
        out_shape=jax.ShapeDtypeStruct((wides, narrows) + shard.shape, shard.dtype),
        in_specs=[hbm],
        out_specs=hbm,
        scratch_shapes=[
            pltpu.SemaphoreType.DMA,
            pltpu.SemaphoreType.DMA((wides - 1,)),
            pltpu.SemaphoreType.DMA((wides, half - 1)),
            pltpu.SemaphoreType.DMA((wides, half)),
            pltpu.SemaphoreType.DMA((wides, narrows)),
        ],
        compiler_params=pltpu.CompilerParams(collective_id=0, has_side_effects=True),
        name="gather_shared",
    )(shard)


def norm_rows(extra, experts):
    turned = jnp.transpose(extra.astype(F32))
    return turned[experts : experts + 4] + turned[experts + 4 : experts + 8] + turned[experts + 8 : experts + 12]


def fwd_kernel(experts, slot_ref, x_ref, wts_ref, qkv_ref, o_ref, lse_ref, hid_ref, u_ref, lse_col, nrm_ref):
    length, width = x_ref.shape[1:]
    blocks = length // ROWS
    head = width // HEADS
    scale = 1.0 / math.sqrt(head)
    wq = wts_ref.at[:, pl.ds(0, 3 * width)]
    wo = wts_ref.at[:, pl.ds(3 * width, width)]
    nrm_ref[0:4, :] = norm_rows(wts_ref[:, 4 * width :], experts)

    def project(i, _):
        at = pl.ds(i * ROWS, ROWS)
        xhat, _ = norm_stats(x_ref[0, at, :].astype(F32))
        al = (xhat * nrm_ref[0:1, :] + nrm_ref[1:2, :]).astype(BF)
        qkv_ref[0, at, :] = dot(al, wq[...], 1, 0).astype(BF)
        return 0

    lax.fori_loop(0, blocks, project, 0)
    lse_col[...] = jnp.zeros_like(lse_col)
    lane = lax.broadcasted_iota(jnp.int32, (1, LANES), 1)
    keep = lax.broadcasted_iota(jnp.int32, (ROWS, ROWS), 1) <= lax.broadcasted_iota(jnp.int32, (ROWS, ROWS), 0)
    for i in range(blocks):
        keys = (i + 1) * ROWS
        at = pl.ds(i * ROWS, ROWS)

        def pair(hp, _, i=i, keys=keys, at=at):
            lanes = pl.ds(pl.multiple_of(hp * LANES, LANES), LANES)
            klanes = pl.ds(pl.multiple_of(hp * LANES + width, LANES), LANES)
            vlanes = pl.ds(pl.multiple_of(hp * LANES + 2 * width, LANES), LANES)
            q = qkv_ref[0, at, lanes]
            k = qkv_ref[0, pl.ds(0, keys), klanes]
            v = qkv_ref[0, pl.ds(0, keys), vlanes]
            acc = None
            for h in range(2):
                mine = lane // head == h
                qm = jnp.where(mine, q * scale, 0).astype(BF)
                vm = jnp.where(mine, v, 0).astype(BF)
                s = dot(qm, k, 1, 1)
                diag = jnp.where(keep, s[:, i * ROWS :], NEG_LARGE)
                s = diag if i == 0 else jnp.concatenate([s[:, : i * ROWS], diag], axis=1)
                m = jnp.max(s, axis=1, keepdims=True)
                p = jnp.exp(s - m)
                total = jnp.sum(p, axis=1, keepdims=True)
                part = dot((p * (1.0 / total)).astype(BF), vm, 1, 0)
                acc = part if acc is None else acc + part
                lse_col[at, :] = jnp.where(lane == hp * 2 + h, m + jnp.log(total), lse_col[at, :])
            o_ref[0, at, lanes] = acc.astype(BF)
            return 0

        lax.fori_loop(0, HEADS // 2, pair, 0)
    lse_ref[0] = jnp.transpose(lse_col[...])[:HEADS, :]

    def finish(i, _):
        at = pl.ds(i * ROWS, ROWS)
        hidden = x_ref[0, at, :].astype(F32) + dot(o_ref[0, at, :], wo[...], 1, 0)
        hid_ref[0, at, :] = hidden
        xhat, _ = norm_stats(hidden)
        u_ref[0, at, :] = (xhat * nrm_ref[2:3, :] + nrm_ref[3:4, :]).astype(BF)
        return 0

    lax.fori_loop(0, blocks, finish, 0)


def whole_spec(shape):
    return pl.BlockSpec(shape, lambda i, s: (0,) * len(shape))


def each_spec(*shape):
    return pl.BlockSpec((1,) + shape, lambda i, s: (i,) + (0,) * len(shape))


def attend(slots, tokens, wts, experts):
    count, length, width = tokens.shape
    return pl.pallas_call(
        functools.partial(fwd_kernel, experts),
        grid_spec=pltpu.PrefetchScalarGridSpec(
            num_scalar_prefetch=1,
            grid=(count,),
            in_specs=[pl.BlockSpec((1, length, width), lambda i, s: (s[i], 0, 0)), whole_spec(wts.shape)],
            out_specs=[
                each_spec(length, 3 * width),
                each_spec(length, width),
                each_spec(HEADS, length),
                each_spec(length, width),
                each_spec(length, width),
            ],
            scratch_shapes=[pltpu.VMEM((length, LANES), F32), pltpu.VMEM((8, width), F32)],
        ),
        out_shape=[
            jax.ShapeDtypeStruct((count, length, 3 * width), BF),
            jax.ShapeDtypeStruct((count, length, width), BF),
            jax.ShapeDtypeStruct((count, HEADS, length), F32),
            jax.ShapeDtypeStruct((count, length, width), F32),
            jax.ShapeDtypeStruct((count, length, width), BF),
        ],
        compiler_params=pltpu.CompilerParams(vmem_limit_bytes=56 << 20),
        name="attention",
    )(slots, tokens, wts)


def bwd_kernel(experts, slot_ref, x_ref, cf_ref, md_ref, hid_ref, qkv_ref, o_ref, lse_ref, wts_ref,
               gt_ref, out_ref, dwq_ref, dwo_ref, dex_ref, dh_ref, do_ref, dqkv_ref, dk_ref, dv_ref, nrm_ref, dn_ref):
    length, width = x_ref.shape[1:]
    blocks = length // ROWS
    part = md_ref.shape[3]
    parts = ROWS // part
    head = width // HEADS
    scale = 1.0 / math.sqrt(head)
    wq = wts_ref.at[:, pl.ds(0, 3 * width)]
    wo = wts_ref.at[:, pl.ds(3 * width, width)]
    nrm_ref[0:4, :] = norm_rows(wts_ref[:, 4 * width :], experts)

    @pl.when(pl.program_id(0) == 0)
    def _():
        dwq_ref[...] = jnp.zeros_like(dwq_ref)
        dwo_ref[...] = jnp.zeros_like(dwo_ref)
        dn_ref[...] = jnp.zeros_like(dn_ref)

    def first(i, _):
        at = pl.ds(i * ROWS, ROWS)
        hidden = hid_ref[0, at, :]
        mix = md_ref[0, pl.ds(i * parts, parts), 0].reshape(ROWS, width).astype(F32)
        out_ref[0, at, :] = (hidden + mix).astype(BF)
        xhat, rstd = norm_stats(hidden)
        du = md_ref[0, pl.ds(i * parts, parts), 1].reshape(ROWS, width).astype(F32)
        dn_ref[2:3, :] += jnp.sum(du * xhat, axis=0, keepdims=True)
        dn_ref[3:4, :] += jnp.sum(du, axis=0, keepdims=True)
        dh = cf_ref[0, at, :].astype(F32) + norm_back(du, nrm_ref[2:3, :], xhat, rstd)
        dh_ref[at, :] = dh
        db = dh.astype(BF)
        do_ref[at, :] = dot(db, wo[...], 1, 1).astype(BF)
        dwo_ref[...] += dot(o_ref[0, at, :], db, 0, 0)
        return 0

    lax.fori_loop(0, blocks, first, 0)
    lane = lax.broadcasted_iota(jnp.int32, (1, LANES), 1)
    keep = lax.broadcasted_iota(jnp.int32, (ROWS, ROWS), 0) <= lax.broadcasted_iota(jnp.int32, (ROWS, ROWS), 1)

    def pair(hp, _):
        lanes = pl.ds(pl.multiple_of(hp * LANES, LANES), LANES)
        klanes = pl.ds(pl.multiple_of(hp * LANES + width, LANES), LANES)
        vlanes = pl.ds(pl.multiple_of(hp * LANES + 2 * width, LANES), LANES)
        for i in range(blocks):
            keys = (i + 1) * ROWS
            at = pl.ds(i * ROWS, ROWS)
            q = qkv_ref[0, at, lanes]
            k = qkv_ref[0, pl.ds(0, keys), klanes]
            v = qkv_ref[0, pl.ds(0, keys), vlanes]
            do = do_ref[at, lanes]
            dq = dk = dv = None
            for h in range(2):
                mine = lane // head == h
                qm = jnp.where(mine, q * scale, 0).astype(BF)
                dom = jnp.where(mine, do, 0).astype(BF)
                km = jnp.where(mine, k * scale, 0).astype(BF)
                s = dot(k, qm, 1, 1)
                s = s - lse_ref[0, pl.ds(hp * 2 + h, 1), at]
                diag = jnp.where(keep, s[i * ROWS :], NEG_LARGE)
                p = jnp.exp(diag if i == 0 else jnp.concatenate([s[: i * ROWS], diag], axis=0))
                pdp = p * dot(v, dom, 1, 1)
                inner = jnp.sum(pdp, axis=0, keepdims=True)
                ds = (pdp - p * inner).astype(BF)
                a = dot(p.astype(BF), dom, 1, 0)
                b = dot(ds, qm, 1, 0)
                c = dot(ds, km, 0, 0)
                dv, dk, dq = (a, b, c) if h == 0 else (dv + a, dk + b, dq + c)
            dqkv_ref[at, lanes] = dq.astype(BF)
            if i:
                dk_ref[: i * ROWS, :] += dk[: i * ROWS]
                dv_ref[: i * ROWS, :] += dv[: i * ROWS]
            dk_ref[i * ROWS : keys, :] = dk[i * ROWS :]
            dv_ref[i * ROWS : keys, :] = dv[i * ROWS :]
        dqkv_ref[:, klanes] = dk_ref[...].astype(BF)
        dqkv_ref[:, vlanes] = dv_ref[...].astype(BF)
        return 0

    lax.fori_loop(0, HEADS // 2, pair, 0)

    def last(i, _):
        at = pl.ds(i * ROWS, ROWS)
        xhat, rstd = norm_stats(x_ref[0, at, :].astype(F32))
        al = (xhat * nrm_ref[0:1, :] + nrm_ref[1:2, :]).astype(BF)
        dqkv = dqkv_ref[at, :]
        dwq_ref[...] += dot(al, dqkv, 0, 0)
        da = dot(dqkv, wq[...], 1, 1)
        dn_ref[0:1, :] += jnp.sum(da * xhat, axis=0, keepdims=True)
        dn_ref[1:2, :] += jnp.sum(da, axis=0, keepdims=True)
        gt_ref[0, at, :] = dh_ref[at, :] + norm_back(da, nrm_ref[0:1, :], xhat, rstd)
        return 0

    lax.fori_loop(0, blocks, last, 0)

    @pl.when(pl.program_id(0) == pl.num_programs(0) - 1)
    def _():
        stacked = jnp.concatenate([dn_ref[...], jnp.zeros((LANES - 8, width), F32)], axis=0)
        dex_ref[...] = jnp.transpose(stacked)


def attend_back(slots, tokens, cot, moved, hid, qkv, o, lse, wts, experts):
    count, length, width = tokens.shape
    slot = pl.BlockSpec((1, length, width), lambda i, s: (s[i], 0, 0))
    return pl.pallas_call(
        functools.partial(bwd_kernel, experts),
        grid_spec=pltpu.PrefetchScalarGridSpec(
            num_scalar_prefetch=1,
            grid=(count,),
            in_specs=[
                slot,
                slot,
                each_spec(*moved.shape[1:]),
                each_spec(length, width),
                each_spec(length, 3 * width),
                each_spec(length, width),
                each_spec(HEADS, length),
                whole_spec(wts.shape),
            ],
            out_specs=[
                slot,
                slot,
                whole_spec((width, 3 * width)),
                whole_spec((width, width)),
                whole_spec((width, LANES)),
            ],
            scratch_shapes=[
                pltpu.VMEM((length, width), F32),
                pltpu.VMEM((length, width), BF),
                pltpu.VMEM((length, 3 * width), BF),
                pltpu.VMEM((length, LANES), F32),
                pltpu.VMEM((length, LANES), F32),
                pltpu.VMEM((8, width), F32),
                pltpu.VMEM((8, width), F32),
            ],
        ),
        out_shape=[
            jax.ShapeDtypeStruct((count, length, width), F32),
            jax.ShapeDtypeStruct((count, length, width), BF),
            jax.ShapeDtypeStruct((width, 3 * width), F32),
            jax.ShapeDtypeStruct((width, width), F32),
            jax.ShapeDtypeStruct((width, LANES), F32),
        ],
        compiler_params=pltpu.CompilerParams(vmem_limit_bytes=60 << 20),
        name="attention_back",
    )(slots, tokens, cot, moved, hid, qkv, o, lse, wts)


def expert_kernel(narrows, counts, u_ref, cf_ref, live_ref, wc_ref, upd_ref,
                  md_ref, grad_ref, dwc_ref,
                  in_buf, xd_out, xd_in, yx_out, yx_in, md_out, w_buf, du_buf, dw_buf, up_buf, down_buf, dup, ddown,
                  load_sem, send_sem, recv_sem):
    w_id, me = lax.axis_index("wide"), lax.axis_index("narrow")
    micros, length, width = counts
    part = length // narrows
    chunk_parts = ROWS // part
    hidden_width = up_buf.shape[1]
    wides = upd_ref.shape[0]
    up_rows = width // wides
    down_rows = hidden_width // wides
    folds = hidden_width // width
    fold_rows = down_rows // folds
    lane = lax.broadcasted_iota(jnp.int32, (1, LANES), 1)

    loads = []
    for j in range(wides):
        loads.append(pltpu.make_async_copy(
            upd_ref.at[j, pl.ds(0, up_rows)], up_buf.at[pl.ds(j * up_rows, up_rows)], load_sem.at[j, 0]))
        for c in range(folds):
            loads.append(pltpu.make_async_copy(
                upd_ref.at[j, pl.ds(up_rows, fold_rows), pl.ds(c * width, width)],
                down_buf.at[pl.ds(j * down_rows + c * fold_rows, fold_rows)], load_sem.at[j, 1 + c]))
    for copy in loads:
        copy.start()
    greet([(w_id, lax.rem(me + k, narrows)) for k in range(1, narrows)])
    dup[...] = jnp.zeros_like(dup)
    ddown[...] = jnp.zeros_like(ddown)
    dwc_ref[...] = jnp.zeros_like(dwc_ref)

    def send(stage, mb, source, target, peer):
        @pl.when(peer != me)
        def _():
            remote(source, target, send_sem.at[stage, mb, peer], recv_sem.at[stage, mb, me], (w_id, peer)).start()

        @pl.when(peer == me)
        def _():
            pltpu.make_async_copy(source, target, recv_sem.at[stage, mb, me]).start()

    def received(stage, mb, peer, target):
        pltpu.make_async_copy(target, target, recv_sem.at[stage, mb, peer]).wait()

    def sent(stage, mb, source):
        def one(k, _):
            peer = lax.rem(me + k, narrows)
            pltpu.make_async_copy(source, source, send_sem.at[stage, mb, peer]).wait()
            return 0

        lax.fori_loop(1, narrows, one, 0)

    def send_rows(mb):
        def one(k, _):
            peer = lax.rem(me + k, narrows)
            rows = pl.ds(peer * part, part)
            send(0, mb, u_ref.at[mb, rows], in_buf.at[mb, me, 0], peer)
            send(1, mb, cf_ref.at[mb, rows], in_buf.at[mb, me, 1], peer)
            return 0

        lax.fori_loop(0, narrows, one, 0)

    def mix(mb):
        def logits(n, _):
            received(0, mb, n, in_buf.at[mb, n, 0])
            received(1, mb, n, in_buf.at[mb, n, 1])
            w_buf[mb, n] = dot(in_buf[mb, n, 0], wc_ref[...], 1, 0).astype(BF).astype(F32)
            return 0

        lax.fori_loop(0, narrows, logits, 0)

        def rows_of(c, _):
            at = pl.ds(c * 16, 16)
            logit = [
                jnp.where(live_ref[mb, pl.ds(n, 1), :] > 0, w_buf[mb, n, at, :], NEG_LARGE) for n in range(narrows)
            ]
            top = functools.reduce(jnp.maximum, logit)
            exps = [jnp.exp(logit[n] - top) * live_ref[mb, pl.ds(n, 1), :] for n in range(narrows)]
            total = functools.reduce(jnp.add, exps)
            inverse = 1.0 / total
            weights = [e * inverse for e in exps]
            for n in range(narrows):
                w_buf[mb, n, at, :] = weights[n]
            for which in range(2):
                values = [in_buf[mb, n, which, at, :].astype(F32) for n in range(narrows)]
                for e in range(narrows):
                    acc = functools.reduce(
                        jnp.add, [weights[n][:, e : e + 1] * values[n] for n in range(narrows)])
                    xd_out[mb, e, which, at, :] = acc.astype(BF)
            return 0

        lax.fori_loop(0, part // 16, rows_of, 0)

        def one(k, _):
            peer = lax.rem(me + k, narrows)
            send(2, mb, xd_out.at[mb, peer], xd_in.at[mb, me], peer)
            return 0

        lax.fori_loop(0, narrows, one, 0)

    def expert(mb):
        def chunk(c, _):
            at = pl.ds(c * chunk_parts, chunk_parts)
            for k in range(chunk_parts):
                received(2, mb, c * chunk_parts + k, xd_in.at[mb, c * chunk_parts + k])
            x = xd_in[mb, at, 0].reshape(ROWS, width)
            dy = xd_in[mb, at, 1].reshape(ROWS, width)

            def tile(j, carry):
                y, dx = carry
                cols = pl.ds(pl.multiple_of(j * width, width), width)
                z = dot(x, up_buf[:, cols], 1, 0)
                zz = z * z
                t = jnp.tanh(GELU_A * (z + GELU_B * z * zz))
                ga = (0.5 * z * (1.0 + t)).astype(BF)
                slope = 0.5 * (1.0 + t) + (0.5 * GELU_A) * z * (1.0 - t * t) * (1.0 + (3.0 * GELU_B) * zz)
                y = y + dot(ga, down_buf[cols, :], 1, 0)
                dz = (dot(dy, down_buf[cols, :], 1, 1) * slope).astype(BF)
                dx = dx + dot(dz, up_buf[:, cols], 1, 1)
                ddown[cols, :] += dot(ga, dy, 0, 0)
                dup[:, cols] += dot(x, dz, 0, 0)
                return y, dx

            zero = jnp.zeros((ROWS, width), F32)
            y, dx = lax.fori_loop(0, folds, tile, (zero, zero))
            yx_out[mb, at, 0] = y.astype(BF).reshape(chunk_parts, part, width)
            yx_out[mb, at, 1] = dx.astype(BF).reshape(chunk_parts, part, width)
            for k in range(chunk_parts):
                peer = c * chunk_parts + k
                send(3, mb, yx_out.at[mb, peer], yx_in.at[mb, me], peer)
            return 0

        lax.fori_loop(0, length // ROWS, chunk, 0)

    def combine(mb):
        def wait(e, _):
            received(3, mb, e, yx_in.at[mb, e])
            return 0

        lax.fori_loop(0, narrows, wait, 0)

        def member(n, _):
            def rows_of(c, _):
                at = pl.ds(c * 16, 16)
                u = in_buf[mb, n, 0, at, :].astype(F32)
                cf = in_buf[mb, n, 1, at, :].astype(F32)
                weights = w_buf[mb, n, at, :]
                mixed = du = None
                dw = jnp.zeros((16, LANES), F32)
                for e in range(narrows):
                    y = yx_in[mb, e, 0, at, :].astype(F32)
                    dx = yx_in[mb, e, 1, at, :].astype(F32)
                    weight = weights[:, e : e + 1]
                    mixed = weight * y if e == 0 else mixed + weight * y
                    du = weight * dx if e == 0 else du + weight * dx
                    dw = jnp.where(lane == e, jnp.sum(dx * u + cf * y, axis=1, keepdims=True), dw)
                md_out[mb, n, 0, at, :] = mixed.astype(BF)
                du_buf[n, at, :] = du
                dw_buf[n, at, :] = dw
                return 0

            lax.fori_loop(0, part // 16, rows_of, 0)
            return 0

        lax.fori_loop(0, narrows, member, 0)

        def group(n, acc):
            return acc + w_buf[mb, n] * dw_buf[n]

        inner = lax.fori_loop(0, narrows, group, jnp.zeros((part, LANES), F32))

        def finish(n, _):
            dc = (w_buf[mb, n] * (dw_buf[n] - inner)).astype(BF)
            du = du_buf[n] + dot(dc, wc_ref[...], 1, 1)
            md_out[mb, n, 1] = du.astype(BF)
            dwc_ref[...] += dot(in_buf[mb, n, 0], dc, 0, 0)
            send(4, mb, md_out.at[mb, n], md_ref.at[mb, me], n)
            return 0

        lax.fori_loop(0, narrows, finish, 0)

    send_rows(0)
    for copy in loads:
        copy.wait()
    for mb in range(micros):
        if mb + 1 < micros:
            send_rows(mb + 1)
        mix(mb)
    for mb in range(micros):
        expert(mb)
    for mb in range(micros):
        combine(mb)
    for j in range(wides):
        grad_ref[j, :up_rows] = dup[j * up_rows : (j + 1) * up_rows].astype(BF)
        for c in range(folds):
            rows = j * down_rows + c * fold_rows
            grad_ref[j, up_rows:, c * width : (c + 1) * width] = ddown[rows : rows + fold_rows].astype(BF)
    for mb in range(micros):
        def wait(p, _, mb=mb):
            received(4, mb, p, md_ref.at[mb, p])
            return 0

        lax.fori_loop(0, narrows, wait, 0)
        sent(0, mb, in_buf.at[mb, 0, 0])
        sent(1, mb, in_buf.at[mb, 0, 1])
        sent(2, mb, xd_out.at[mb, 0])
        sent(3, mb, yx_out.at[mb, 0])
        sent(4, mb, md_out.at[mb, 0])


def run_experts(u, cf, live, wc, upd, narrows):
    micros, length, width = u.shape
    part = length // narrows
    wides, packed_rows, hidden_width = upd.shape
    folds = hidden_width // width
    hbm = pl.BlockSpec(memory_space=pl.ANY)
    vmem = pl.BlockSpec(memory_space=pltpu.VMEM)
    pairs = pltpu.VMEM((micros, narrows, 2, part, width), BF)
    return pl.pallas_call(
        functools.partial(expert_kernel, narrows, (micros, length, width)),
        out_shape=[
            jax.ShapeDtypeStruct((micros, narrows, 2, part, width), BF),
            jax.ShapeDtypeStruct(upd.shape, BF),
            jax.ShapeDtypeStruct((width, LANES), F32),
        ],
        in_specs=[hbm, hbm, vmem, vmem, hbm],
        out_specs=[hbm, vmem, vmem],
        scratch_shapes=[pairs] * 6 + [
            pltpu.VMEM((micros, narrows, part, LANES), F32),
            pltpu.VMEM((narrows, part, width), F32),
            pltpu.VMEM((narrows, part, LANES), F32),
            pltpu.VMEM((width, hidden_width), BF),
            pltpu.VMEM((hidden_width, width), BF),
            pltpu.VMEM((width, hidden_width), F32),
            pltpu.VMEM((hidden_width, width), F32),
            pltpu.SemaphoreType.DMA((wides, 1 + folds)),
            pltpu.SemaphoreType.DMA((5, micros, narrows)),
            pltpu.SemaphoreType.DMA((5, micros, narrows)),
        ],
        compiler_params=pltpu.CompilerParams(
            collective_id=1, has_side_effects=True, vmem_limit_bytes=62 << 20),
        name="experts",
    )(u, cf, live, wc, upd)


def reduce_kernel(wides, narrows, wq_ref, wo_ref, ex_ref, dwc_ref, out_ref,
                  s1, r1, s2, r2, s3, r3, total, c_sem, p_sem, z_sem, cr_sem, pr_sem, zr_sem):
    w, n = lax.axis_index("wide"), lax.axis_index("narrow")
    half = narrows // 2
    q, parity = n // 2, lax.rem(n, 2)
    core = n + 1 - 2 * parity
    z_peers = [lax.rem(w + k, wides) for k in range(1, wides)]
    p_peers = [lax.rem(q + k, half) for k in range(1, half)]
    greet([(w, core)] + [(w, p * 2 + parity) for p in p_peers] + [(z, n) for z in z_peers])
    a, b = wq_ref.shape[2], wq_ref.shape[2] + wo_ref.shape[2]

    def parts(index):
        return wq_ref[index], wo_ref[index], ex_ref[index] + dwc_ref[index]

    sends = []
    for k in range(half):
        there = lax.rem(q + 1 + k, half)

        def fill(z, _, there=there):
            one, two, three = parts(z * narrows + 2 * there + 1 - parity)
            s1[there, z, :, :a] = one.astype(BF)
            s1[there, z, :, a:b] = two.astype(BF)
            s1[there, z, :, b:] = three.astype(BF)
            return 0

        lax.fori_loop(0, wides, fill, 0)
        copy = remote(s1.at[there], r1.at[there], c_sem.at[k], cr_sem.at[there], (w, core))
        copy.start()
        sends.append(copy)
    for k in range(half):
        there = lax.rem(q + 1 + k, half)
        remote(s1.at[there], r1.at[there], c_sem.at[k], cr_sem.at[there], (w, core)).wait_recv()
        last = k == half - 1

        def add(z, _, there=there, last=last):
            one, two, three = parts(z * narrows + 2 * there + parity)
            got = r1[there, z].astype(F32)
            one, two, three = one + got[:, :a], two + got[:, a:b], three + got[:, b:]
            if last:
                total[z, :, :a], total[z, :, a:b], total[z, :, b:] = one, two, three
            else:
                s2[there, z, :, :a] = one.astype(BF)
                s2[there, z, :, a:b] = two.astype(BF)
                s2[there, z, :, b:] = three.astype(BF)
            return 0

        lax.fori_loop(0, wides, add, 0)
        if not last:
            copy = remote(s2.at[there], r2.at[q], p_sem.at[k], pr_sem.at[q], (w, there * 2 + parity))
            copy.start()
            sends.append(copy)
    for k in range(1, half):
        there = lax.rem(q + k, half)
        remote(s2.at[there], r2.at[there], p_sem.at[0], pr_sem.at[there], (w, n)).wait_recv()
    for k in range(wides):
        z = lax.rem(w + 1 + k, wides)
        acc = total[z]
        for i in range(1, half):
            acc = acc + r2[lax.rem(q + i, half), z].astype(F32)
        if k < wides - 1:
            s3[z] = acc.astype(BF)
            copy = remote(s3.at[z], r3.at[w], z_sem.at[k], zr_sem.at[w], (z, n))
            copy.start()
            sends.append(copy)
        else:
            out_ref[...] = acc
    for k in range(1, wides):
        z = lax.rem(w + k, wides)
        remote(s3.at[z], r3.at[z], z_sem.at[0], zr_sem.at[z], (w, n)).wait_recv()
        out_ref[...] += r3[z].astype(F32)
    for copy in sends:
        copy.wait_send()


def reduce_shared(dwq, dwo, dex, dwc, wides, narrows):
    half = narrows // 2
    rows = dwq.shape[1]
    cols = dwq.shape[2] + dwo.shape[2] + dex.shape[2]
    vmem = pl.BlockSpec(memory_space=pltpu.VMEM)
    block = (half, wides, rows, cols)
    sems = pltpu.SemaphoreType.DMA
    return pl.pallas_call(
        functools.partial(reduce_kernel, wides, narrows),
        out_shape=jax.ShapeDtypeStruct((rows, cols), F32),
        in_specs=[vmem] * 4,
        out_specs=vmem,
        scratch_shapes=[pltpu.VMEM(block, BF)] * 4
        + [pltpu.VMEM(block[1:], BF)] * 2
        + [pltpu.VMEM(block[1:], F32)]
        + [sems((half,)), sems((half,)), sems((wides,))] * 2,
        compiler_params=pltpu.CompilerParams(
            collective_id=2, has_side_effects=True, vmem_limit_bytes=60 << 20),
        name="reduce_shared",
    )(dwq, dwo, dex, dwc)


def total_kernel(wides, narrows, part_ref, out_ref, got_n, mid, got_w, send_n, recv_n, send_w, recv_w):
    w, n = lax.axis_index("wide"), lax.axis_index("narrow")
    n_peers = [lax.rem(n + k, narrows) for k in range(1, narrows)]
    z_peers = [lax.rem(w + k, wides) for k in range(1, wides)]
    greet([(w, p) for p in n_peers] + [(z, n) for z in z_peers])
    sends = []
    for k, p in enumerate(n_peers):
        copy = remote(part_ref, got_n.at[n], send_n.at[k], recv_n.at[n], (w, p))
        copy.start()
        sends.append(copy)
    got_n[n] = part_ref[...]
    for p in n_peers:
        remote(part_ref, got_n.at[p], send_n.at[0], recv_n.at[p], (w, n)).wait_recv()
    acc = got_n[0]
    for k in range(1, narrows):
        acc = acc + got_n[k]
    mid[...] = acc
    got_w[w] = acc
    for k, z in enumerate(z_peers):
        copy = remote(mid, got_w.at[w], send_w.at[k], recv_w.at[w], (z, n))
        copy.start()
        sends.append(copy)
    for z in z_peers:
        remote(mid, got_w.at[z], send_w.at[0], recv_w.at[z], (w, n)).wait_recv()
    acc = got_w[0]
    for k in range(1, wides):
        acc = acc + got_w[k]
    out_ref[...] = acc
    for copy in sends:
        copy.wait_send()


def sum_everywhere(part, wides, narrows):
    vmem = pl.BlockSpec(memory_space=pltpu.VMEM)
    sems = pltpu.SemaphoreType.DMA
    return pl.pallas_call(
        functools.partial(total_kernel, wides, narrows),
        out_shape=jax.ShapeDtypeStruct(part.shape, F32),
        in_specs=[vmem],
        out_specs=vmem,
        scratch_shapes=[
            pltpu.VMEM((narrows,) + part.shape, F32),
            pltpu.VMEM(part.shape, F32),
            pltpu.VMEM((wides,) + part.shape, F32),
            sems((narrows - 1,)),
            sems((narrows,)),
            sems((wides - 1,)),
            sems((wides,)),
        ],
        compiler_params=pltpu.CompilerParams(collective_id=3, has_side_effects=True),
        name="sum_everywhere",
    )(part)


def adam_update(weight, first_state, second_state, gradient, factor, rate, decay):
    clipped = gradient * factor
    first_new = BETA_ONE * first_state + (1.0 - BETA_ONE) * clipped
    second_new = BETA_TWO * second_state + (1.0 - BETA_TWO) * clipped * clipped
    first_hat = first_new / (1.0 - BETA_ONE**STEP)
    second_hat = second_new / (1.0 - BETA_TWO**STEP)
    weight_new = weight - rate * (first_hat / (jnp.sqrt(second_hat) + ADAM_EPS) + decay * weight)
    return (weight_new, first_new, second_new, weight_new.astype(BF))


def per_device(
    tokens, cotangent, seq_counts, micro_assign,
    norm_params, norm_first, norm_second,
    project_weight, project_first, project_second,
    output_weight, output_first, output_second,
    control_weight, control_first, control_second,
    up_weight, up_first, up_second,
    down_weight, down_first, down_second,
):
    wides, narrows = lax.axis_size("wide"), lax.axis_size("narrow")
    wide_index, narrow_index = lax.axis_index("wide"), lax.axis_index("narrow")
    devices = wides * narrows
    micro_count, length, width = tokens.shape
    experts = control_weight.shape[1]
    rows = project_weight.shape[0]
    padded = max(rows, 16)
    hidden_width = up_weight.shape[2]
    folds = hidden_width // width

    first_device = wide_index * narrows
    row_counts = lax.dynamic_slice_in_dim(seq_counts, first_device, narrows)
    row_assign = lax.dynamic_slice_in_dim(micro_assign, first_device, narrows, 0)
    slot_numbers = jnp.arange(micro_count, dtype=jnp.int32)
    micros = jnp.arange(micro_count, dtype=jnp.int32)
    member_slots = jnp.sum(
        slot_numbers[None, None, :] * (row_assign[None] == micros[:, None, None]).astype(jnp.int32), axis=2
    )
    live = (member_slots < row_counts[None]).astype(F32)
    live = jnp.broadcast_to(live[:, :, None], (micro_count, narrows, LANES))
    slots = lax.dynamic_index_in_dim(member_slots, narrow_index, 1, keepdims=False)

    norm_turned = norm_params.T
    high = lax.reduce_precision(norm_turned, 8, 7)
    middle = lax.reduce_precision(norm_turned - high, 8, 7)
    lower = norm_turned - high - middle
    extra = jnp.concatenate([control_weight, high, middle, lower], axis=1).astype(BF)
    extra = jnp.pad(extra, ((0, 0), (0, LANES - extra.shape[1])))
    shard = jnp.concatenate([project_weight.astype(BF), output_weight.astype(BF), extra], axis=1)
    shard = jnp.pad(shard, ((0, padded - rows), (0, 0)))
    wts = gather_shared(shard, wides, narrows).reshape(devices, padded, -1)[:, :rows].reshape(width, -1)

    down_rows = down_weight.shape[1]
    fold_rows = down_rows // folds
    down_folded = down_weight[0].reshape(folds, fold_rows, width).transpose(1, 0, 2).reshape(fold_rows, hidden_width)
    packed = jnp.concatenate([up_weight[0], down_folded], axis=0).astype(BF)
    upd = lax.all_gather(packed, "wide", axis=0, tiled=False)

    qkv, o, lse, hid, u = attend(slots, tokens, wts, experts)
    cf = jnp.stack([lax.dynamic_index_in_dim(cotangent, slots[k], 0, keepdims=False) for k in range(micro_count)])
    wc = jnp.where(jnp.arange(LANES)[None, :] < experts, wts[:, 4 * width :], 0)
    moved, grads, dwc = run_experts(u, cf, live, wc, upd, narrows)
    expert_grad = lax.psum_scatter(grads, "wide", scatter_dimension=0, tiled=False).astype(F32)

    grad_tokens, out_rows, dwq, dwo, dex = attend_back(
        slots, tokens, cotangent, moved, hid, qkv, o, lse, wts, experts)
    dex = jnp.roll(dex, experts, axis=1)

    def by_owner(grad):
        return jnp.pad(grad.reshape(devices, rows, -1), ((0, 0), (0, padded - rows), (0, 0)))

    shared = reduce_shared(by_owner(dwq), by_owner(dwo), by_owner(dex), by_owner(dwc), wides, narrows)[:rows]
    project_grad = shared[:, : 3 * width]
    output_grad = shared[:, 3 * width : 4 * width]
    control_grad = shared[:, 4 * width : 4 * width + experts]
    norm_grad = shared[:, 4 * width + experts : 4 * width + experts + 4].T
    up_rows = up_weight.shape[1]
    up_grad = expert_grad[None, :up_rows]
    down_grad = (
        expert_grad[up_rows:].reshape(fold_rows, folds, width).transpose(1, 0, 2).reshape(1, down_rows, width)
    )
    squares = jnp.sum(shared * shared) + jnp.sum(expert_grad * expert_grad)
    total = sum_everywhere(jnp.full((8, LANES), squares, F32), wides, narrows)
    grad_norm = jnp.sqrt(total[0, 0])
    factor = CLIP_NORM / jnp.maximum(grad_norm, CLIP_NORM)
    norm_out = adam_update(norm_params, norm_first, norm_second, norm_grad, factor, 0.3, 0.0)
    project_out = adam_update(
        project_weight, project_first, project_second, project_grad, factor, 0.03, DECAY_RATE)
    output_out = adam_update(output_weight, output_first, output_second, output_grad, factor, 0.2, DECAY_RATE)
    control_out = adam_update(
        control_weight, control_first, control_second, control_grad, factor, 0.015, DECAY_RATE)
    up_out = adam_update(up_weight, up_first, up_second, up_grad, factor, 0.1, DECAY_RATE)
    down_out = adam_update(down_weight, down_first, down_second, down_grad, factor, 0.1, DECAY_RATE)
    return (out_rows, grad_tokens, grad_norm) + norm_out + project_out + output_out + control_out + up_out + down_out


def solution(mesh):
    both = ("wide", "narrow")
    rows3, cols, rows2, expert = P(both, None, None), P(None, both), P(both, None), P("narrow", "wide", None)
    return jax.shard_map(
        per_device,
        mesh=mesh,
        in_specs=(rows3, rows3, P(), P()) + (cols,) * 3 + (rows2,) * 9 + (expert,) * 6,
        out_specs=(rows3, rows3, P()) + (cols,) * 4 + (rows2,) * 12 + (expert,) * 8,
        check_vma=False,
    )
```

time: 1470 us -> 432 us (0.29)
  waiting for transfers between devices: 697 us -> 6.59 us
  Pallas kernels: 0 us -> 364 us
  matrix products: 249 us -> 0 us
  blocking collectives: 181 us -> 0 us
  local copies, waits for them, and re-layouts: 149 us -> 14.8 us
  other arithmetic: 158 us -> 24.6 us
    pallas_call x0 -> x6, Pallas kernels: none -> 364 us  [the longest x1 188 us: run_experts(): pl.pallas_call(functools.partial(expert_kernel, narrows, (micros, length,...]
    dot_general x56 -> x0, matrix products: 249 us -> none  [the longest x2 30.5 us: per_device(): jnp.einsum('nlx,nld->xld', owned_weights, group_target.astype(jnp.float32...]
    reduce_scatter x4 -> x1, waiting for transfers between devices: 234 us -> 0.01 us  [per_device(): lax.psum_scatter(grads, 'wide', scatter_dimension=0, tiled=False)]
    all_gather x11 -> x1, waiting for transfers between devices: 235 us -> 6.56 us  [per_device(): upd = lax.all_gather(packed, 'wide', axis=0, tiled=False)]
    unnamed x20 -> x2, waiting for transfers between devices: 228 us -> 0.03 us
    all_gather x5 -> x0, blocking collectives: 141 us -> none  [the longest x1 43.5 us: per_device(): lax.all_gather(norm_params, ('wide', 'narrow'), axis=1, tiled=True)]
    unnamed x417 -> x52, local copies, waits for them, and re-layouts: 70.9 us -> 7.87 us
    unnamed x14 -> x0, other arithmetic: 45.4 us -> none
  transfers between devices with their start and end apart: 18 -> 2, of which waited for: 11 -> 1; matrix products, arithmetic and copies ran while one was open for 35% -> 3% of each run, Pallas kernels for 0% -> 38%
where the time goes in v1:
time: 432 us; the launch traced here: 431 us
  Pallas kernels  364 us (84%)
  other arithmetic  24.6 us (6%)
  between operations  21.5 us (5%)
  local copies, waits for them, and re-layouts  14.8 us (3%)
  waiting for transfers between devices  6.59 us (2%)
    pallas_call x1, Pallas kernels, run_experts(): pl.pallas_call(functools.partial(expert_kernel, narrows, (micros, length,...  188 us
    pallas_call x1, Pallas kernels, attend_back(): pl.pallas_call(functools.partial(bwd_kernel, experts), grid_spec=pltpu.Pr...  64.2 us
    pallas_call x1, Pallas kernels, attend(): pl.pallas_call(functools.partial(fwd_kernel, experts), grid_spec=pltpu.Pr...  45.9 us
    pallas_call x1, Pallas kernels, reduce_shared(): pl.pallas_call(functools.partial(reduce_kernel, wides, narrows), out_shap...  29.4 us
    pallas_call x1, Pallas kernels, gather_shared(): pl.pallas_call(functools.partial(gather_kernel, wides, narrows), out_shap...  24.2 us
    pallas_call x1, Pallas kernels, sum_everywhere(): pl.pallas_call(functools.partial(total_kernel, wides, narrows), out_shape...  12.3 us
    convert_element_type x6, other arithmetic, adam_update(): return (weight_new, first_new, second_new, weight_new.astype(BF))  11 us
  transfers between devices with their start and end apart: 2, of which 1 were waited for; matrix products, arithmetic and copies ran while one was open for 3% of the time, Pallas kernels for 38%

profile of v1, /device:TPU:0, one launch (start us, length us, event | category | flops | bytes accessed | tf_op | source)
XLA Modules:
  0.0 431.2 jit_solution(12382153723478460291)
XLA Ops:
  7.3 1.4 convert.26
  9.6 1.1 pad_maximum_fusion.1
  10.8 0.7 fusion.31
  15.6 24.2 %gather_shared.1 = bf16[4,8,16,2176]{3,2,1,0:T(8,128)(2,1)} custom-call(bf16[16,2176]{1,0:T(8,128)(2,1)} %pad_maximum_fusion.3.shard_ref), custom_call_target="tpu_custom_call" | custom-call | tf_op jit(solution)/shard_map/gather_shared/pallas_call | solution.py:106
  41.2 45.9 %attention.1 = (bf16[2,1024,1536]{2,1,0:T(8,128)(2,1)}, bf16[2,1024,512]{2,1,0:T(8,128)(2,1)}, f32[2,8,1024]{2,1,0:T(8,128)}, f32[2,1024,512]{2,1,0:T(8,128)}, bf16[2,1024,512]{2,1,0:T(8,128)(2,1)}) custom-call(s32[2]{0:T(128)} %get-tuple-element.212.slot_ref, bf16[2,1024,512]{2,1,0:T(8,128)(2,1)} %x_ref.3, bf16[512,2176]{1,0:T(8,128)(2,1)} %bitcast.49), custom_call_target="tpu_custom_call" | custom-call | tf_op jit(solution)/shard_map/attention/pallas_call | solution.py:200
  87.3 1.5 pad_maximum_fusion.cf_ref
  88.8 1.6 slice_select_fusion.wc_ref
  90.4 6.6 %all-gather.2.cloned.1.call-done.upd_ref = bf16[4,256,2048]{2,1,0:T(8,128)(2,1)} async-done(((bf16[1,256,2048]{2,1,0:T(8,128)(2,1)}), bf16[4,256,2048]{2,1,0:T(8,128)(2,1)}) %all-gather.2.cloned.1.call-update) | async-done | bytes 4194320 | tf_op jit(solution)/shard_map/all_gather | solution.py:821
  97.6 187.7 %experts.1 = (bf16[2,8,2,128,512]{4,3,2,1,0:T(8,128)(2,1)}, bf16[4,256,2048]{2,1,0:T(8,128)(2,1)}, f32[512,128]{1,0:T(8,128)}) custom-call(bf16[2,1024,512]{2,1,0:T(8,128)(2,1)} %get-tuple-element.40.u_ref, bf16[2,1024,512]{2,1,0:T(8,128)(2,1)} %pad_maximum_fusion.cf_ref, f32[2,8,128]{2,1,0:T(8,128)} %broadcast_in_dim.12.live_ref, ...), custom_call_target="tpu_custom_call" | custom-call | tf_op jit(solution)/shard_map/experts/pallas_call | solution.py:589
  286.6 0.7 copy.146
  287.5 64.2 %attention_back.1 = (f32[2,1024,512]{2,1,0:T(8,128)}, bf16[2,1024,512]{2,1,0:T(8,128)(2,1)}, f32[512,1536]{1,0:T(8,128)}, f32[512,512]{1,0:T(8,128)}, f32[512,128]{1,0:T(8,128)}) custom-call(s32[2]{0:T(128)} %get-tuple-element.212.slot_ref, bf16[2,1024,512]{2,1,0:T(8,128)(2,1)} %x_ref.3, bf16[2,1024,512]{2,1,0:T(8,128)(2,1)} %cf_ref.1, ...), custom_call_target="tpu_custom_call" | custom-call | tf_op jit(solution)/shard_map/attention_back/pallas_call | solution.py:328
  351.6 1.1 slice.45
  352.7 1.8 pad_maximum_fusion.2
  354.5 29.4 %reduce_shared.1 = f32[16,2176]{1,0:T(8,128)} custom-call(f32[32,16,1536]{2,1,0:T(8,128)} %bitcast.54, f32[32,16,512]{2,1,0:T(8,128)} %bitcast.57, f32[32,16,128]{2,1,0:T(8,128)} %bitcast.58, f32[32,16,128]{2,1,0:T(8,128)} %bitcast.60), custom_call_target="tpu_custom_call" | custom-call | tf_op jit(solution)/shard_map/reduce_shared/pallas_call | solution.py:697
  384.0 1.5 multiply_reduce_fusion.1
  385.5 2.5 multiply_reduce_fusion
  389.9 12.3 %sum_everywhere.1 = f32[8,128]{1,0:T(8,128)} custom-call(f32[8,128]{1,0:T(8,128)} %broadcast_in_dim.30.part_ref), custom_call_target="tpu_custom_call" | custom-call | tf_op jit(solution)/shard_map/sum_everywhere/pallas_call | solution.py:747
  402.1 1.2 slice.47
  404.1 1.5 convert_element_type.52
  405.5 3.7 fusion.20
  409.3 0.7 mul.303
  416.1 1.4 fusion.25
  417.5 1.7 fusion.27
  419.1 4.1 fusion.18
  (78 shorter events, 11.6 us)
Async XLA Ops:
  7.2 3.5 copy-start
  7.2 2.2 copy-start.3
  7.2 89.7 %all-gather.2.cloned.1.call-start = ((), (), s32[]{:S(2)}) async-start(), calls=%async_computation.1 | async-start | bytes 5242880 | tf_op jit(solution)/shard_map/all_gather | solution.py:821
  9.5 5.2 %copy-start.15 = (f32[4,16]{1,0:T(4,128)S(1)}, f32[4,16]{1,0:T(4,128)}, u32[]{:S(2)}) copy-start(f32[4,16]{1,0:T(4,128)} %param.26) | copy-start | bytes 772
  9.5 5.3 %copy-start.12 = (f32[16,8]{0,1:T(8,128)S(1)}, f32[16,8]{0,1:T(8,128)}, u32[]{:S(2)}) copy-start(f32[16,8]{0,1:T(8,128)} %param.35) | copy-start | bytes 1540
  9.5 5.3 %copy-start.7 = (f32[16,1536]{1,0:T(8,128)S(1)}, f32[16,1536]{1,0:T(8,128)}, u32[]{:S(2)}) copy-start(f32[16,1536]{1,0:T(8,128)} %param.29) | copy-start | bytes 294916
  9.5 5.3 %copy-start.8 = (f32[16,512]{1,0:T(8,128)S(1)}, f32[16,512]{1,0:T(8,128)}, u32[]{:S(2)}) copy-start(f32[16,512]{1,0:T(8,128)} %param.32) | copy-start | bytes 98308
  10.6 29.2 %copy-start.18 = (s32[32]{0:T(128)S(1)}, s32[32]{0:T(128)}, u32[]{:S(2)}) copy-start(s32[32]{0:T(128)} %param.24) | copy-start | bytes 388
  10.7 374.8 %reduce-scatter.2.cloned.1.call-start = ((), (), s32[]{:S(2)}) async-start(), calls=%async_computation.2 | async-start | bytes 5242880 | tf_op jit(solution)/shard_map/reduce_scatter | solution.py:827
  41.2 45.9 %copy-start.2 = (bf16[2,1024,512]{2,1,0:T(8,128)(2,1)S(1)}, bf16[2,1024,512]{2,1,0:T(8,128)(2,1)}, u32[]{:S(2)}) copy-start(bf16[2,1024,512]{2,1,0:T(8,128)(2,1)} %cf_ref.1) | copy-start | bytes 6291460
  285.3 0.7 copy-start.13
  285.3 1.3 copy-start.14
  285.3 2.0 copy-start.16
  285.3 2.1 copy-start.17
  385.5 20.0 %copy-start.6 = (f32[1,128,2048]{2,1,0:T(8,128)S(1)}, f32[1,128,2048]{2,1,0:T(8,128)}, u32[]{:S(2)}) copy-start(f32[1,128,2048]{2,1,0:T(8,128)} %param.39) | copy-start | bytes 3145732
  409.2 1.1 copy-start.5
  409.3 8.2 %copy-start.9 = (f32[16,1536]{1,0:T(8,128)S(1)}, f32[16,1536]{1,0:T(8,128)}, u32[]{:S(2)}) copy-start(f32[16,1536]{1,0:T(8,128)} %param.30) | copy-start | bytes 294916
  410.0 0.7 copy-start.10
  410.0 0.7 copy-start.11
  410.0 9.2 %copy-start.4 = (f32[1,512,512]{2,1,0:T(8,128)S(1)}, f32[1,512,512]{2,1,0:T(8,128)}, u32[]{:S(2)}) copy-start(f32[1,512,512]{2,1,0:T(8,128)} %param.41) | copy-start | bytes 3145732
  419.1 4.1 copy-start.1
Sparse Core Ops, SparseCore 0:
  10.8 86.0 all-gather.1
  285.5 80.5 reduce-scatter.1

commit v2 on v1

v2 whole, which is shorter than its diff:
```python
import functools
import math

import jax
import jax.numpy as jnp
from jax import lax
from jax.experimental import pallas as pl
from jax.experimental.pallas import tpu as pltpu
from jax.sharding import PartitionSpec as P

HEADS = 8
STEP = 5
NEG_LARGE = -1e30
NORM_EPS = 1e-05
CLIP_NORM = 0.05
BETA_ONE = 0.5
BETA_TWO = 0.5
ADAM_EPS = 1e-08
DECAY_RATE = 0.1

BF = jnp.bfloat16
F32 = jnp.float32
MESH = pl.DeviceIdType.MESH
LANES = 128
ROWS = 256
GELU_A = math.sqrt(2.0 / math.pi)
GELU_B = 0.044715


def dot(a, b, ca, cb):
    return lax.dot_general(a, b, (((ca,), (cb,)), ((), ())), preferred_element_type=F32)


def norm_stats(v):
    centred = v - jnp.mean(v, axis=-1, keepdims=True)
    rstd = lax.rsqrt(jnp.mean(centred * centred, axis=-1, keepdims=True) + NORM_EPS)
    return centred * rstd, rstd


def norm_back(grad, gain, xhat, rstd):
    t = grad * gain
    return rstd * (t - jnp.mean(t, axis=-1, keepdims=True) - xhat * jnp.mean(t * xhat, axis=-1, keepdims=True))


def remote(src, dst, send, recv, device):
    return pltpu.make_async_remote_copy(
        src_ref=src, dst_ref=dst, send_sem=send, recv_sem=recv, device_id=device, device_id_type=MESH
    )


def greet(devices):
    barrier = pltpu.get_barrier_semaphore()
    for device in devices:
        pl.semaphore_signal(barrier, inc=1, device_id=device, device_id_type=MESH)
    pl.semaphore_wait(barrier, len(devices))


def norm_rows(extra, experts):
    turned = jnp.transpose(extra.astype(F32))
    return turned[experts : experts + 4] + turned[experts + 4 : experts + 8] + turned[experts + 8 : experts + 12]


U, CF, XD, YX, DU, MIX = range(6)


def block_kernel(wides, narrows, rows, flag_ref, live_ref, tok_ref, cot_ref, shard_ref, upw_ref, downw_ref,
                 gt_ref, out_ref, dwq_ref, dwo_ref, dex_ref, dwc_ref, ownup_ref, owndown_ref, gotup_ref, gotdown_ref,
                 raw, wts, uc, qkv_buf, o_buf, lse_buf, lse_col, nrm, dn, in_buf, xd_out, xd_in, yx_in, w_buf, dw_buf,
                 wc_buf, up_buf, down_buf, g_buf, dk_ref, dv_ref,
                 gz_sem, gp_sem, gc_sem, gr_sem, hop_sem, hopr_sem, send_sem, recv_sem, rs_sem, rsr_sem, own_sem, io_sem):
    w_id, me = lax.axis_index("wide"), lax.axis_index("narrow")
    micros, length, width = tok_ref.shape
    blocks = length // ROWS
    part = length // narrows
    head = width // HEADS
    scale = 1.0 / math.sqrt(head)
    hidden_width = up_buf.shape[1]
    up_rows = width // wides
    down_rows = hidden_width // wides
    folds = hidden_width // width
    chunk_parts = ROWS // part
    half = narrows // 2
    q_id, parity = me // 2, lax.rem(me, 2)
    core = me + 1 - 2 * parity
    lane = lax.broadcasted_iota(jnp.int32, (1, LANES), 1)
    padded = shard_ref.shape[0]
    wq, wo = wts.at[:, pl.ds(0, 3 * width)], wts.at[:, pl.ds(3 * width, width)]

    def pick(ref, mb, at):
        value = ref[0, at, :].astype(F32)
        for j in range(1, micros):
            chosen = flag_ref[mb * micros + j : mb * micros + j + 1, 0:1] > 0
            value = jnp.where(chosen, ref[j, at, :].astype(F32), value)
        return value

    z_peers = [lax.rem(w_id + k, wides) for k in range(1, wides)]
    p_peers = [lax.rem(q_id + k, half) * 2 + parity for k in range(1, half)]
    greet([(z, me) for z in z_peers] + [(w_id, lax.rem(me + k, narrows)) for k in range(1, narrows)])

    def slot(zw, zn):
        return raw.at[pl.ds(pl.multiple_of((zw * narrows + zn) * padded, padded), padded)]

    own = pltpu.make_async_copy(shard_ref, slot(w_id, me), own_sem.at[0])
    own.start()
    gather_sends = []

    def spread(src, zw, zn, sem, device):
        copy = remote(src, slot(zw, zn), sem, gr_sem.at[zw, zn], device)
        copy.start()
        gather_sends.append(copy)

    def arrived(zw, zn):
        pltpu.make_async_copy(shard_ref, slot(zw, zn), gr_sem.at[zw, zn]).wait()

    for k, z in enumerate(z_peers):
        spread(shard_ref, w_id, me, gz_sem.at[k], (z, me))
    for k, p in enumerate(p_peers):
        spread(shard_ref, w_id, me, gp_sem.at[0, k], (w_id, p))
    spread(shard_ref, w_id, me, gc_sem.at[0, 0], (w_id, core))

    def up_part(z):
        return up_buf.at[pl.ds(pl.multiple_of(z * up_rows, up_rows), up_rows)]

    def down_part(z):
        return down_buf.at[pl.ds(pl.multiple_of(z * down_rows, down_rows), down_rows)]

    up_buf[pl.ds(pl.multiple_of(w_id * up_rows, up_rows), up_rows), :] = upw_ref[...].astype(BF)
    down_buf[pl.ds(pl.multiple_of(w_id * down_rows, down_rows), down_rows), :] = downw_ref[...].astype(BF)

    def hop_send(hop):
        @pl.when((w_id >= hop - 1) & (w_id < wides - 1))
        def _():
            for i, piece in enumerate((up_part, down_part)):
                source = piece(w_id - (hop - 1))
                remote(source, source, hop_sem.at[hop - 1, 0, i], hopr_sem.at[hop - 1, 0, i], (w_id + 1, me)).start()

        @pl.when((w_id + (hop - 1) <= wides - 1) & (w_id > 0))
        def _():
            for i, piece in enumerate((up_part, down_part)):
                source = piece(w_id + (hop - 1))
                remote(source, source, hop_sem.at[hop - 1, 1, i], hopr_sem.at[hop - 1, 1, i], (w_id - 1, me)).start()

    def hop_arrived(hop):
        @pl.when(w_id >= hop)
        def _():
            for i, piece in enumerate((up_part, down_part)):
                target = piece(w_id - hop)
                pltpu.make_async_copy(target, target, hopr_sem.at[hop - 1, 0, i]).wait()

        @pl.when(w_id + hop <= wides - 1)
        def _():
            for i, piece in enumerate((up_part, down_part)):
                target = piece(w_id + hop)
                pltpu.make_async_copy(target, target, hopr_sem.at[hop - 1, 1, i]).wait()

    def hop_sent(hop):
        @pl.when((w_id >= hop - 1) & (w_id < wides - 1))
        def _():
            for i, piece in enumerate((up_part, down_part)):
                source = piece(w_id - (hop - 1))
                pltpu.make_async_copy(source, source, hop_sem.at[hop - 1, 0, i]).wait()

        @pl.when((w_id + (hop - 1) <= wides - 1) & (w_id > 0))
        def _():
            for i, piece in enumerate((up_part, down_part)):
                source = piece(w_id + (hop - 1))
                pltpu.make_async_copy(source, source, hop_sem.at[hop - 1, 1, i]).wait()

    for j in range(1, wides):
        zw = lax.rem(w_id + wides - j, wides)
        arrived(zw, me)
        for k, p in enumerate(p_peers):
            spread(slot(zw, me), zw, me, gp_sem.at[j, k], (w_id, p))
        spread(slot(zw, me), zw, me, gc_sem.at[j, 0], (w_id, core))
    hop_send(1)

    def choose(i, _):
        at = pl.ds(i * ROWS, ROWS)
        for mb in range(micros):
            uc[mb, 1, at, :] = pick(cot_ref, mb, at).astype(BF)
        return 0

    lax.fori_loop(0, blocks, choose, 0)
    dwc_ref[...] = jnp.zeros_like(dwc_ref)
    for i in range(1, half):
        zn = lax.rem(q_id + half - i, half) * 2 + parity
        for j in range(wides):
            zw = lax.rem(w_id + wides - j, wides)
            arrived(zw, zn)
            spread(slot(zw, zn), zw, zn, gc_sem.at[j, i], (w_id, core))

    def send(stage, mb, source, target, peer):
        @pl.when(peer != me)
        def _():
            remote(source, target, send_sem.at[stage, mb, peer], recv_sem.at[stage, mb, me], (w_id, peer)).start()

        @pl.when(peer == me)
        def _():
            pltpu.make_async_copy(source, target, recv_sem.at[stage, mb, me]).start()

    def received(stage, mb, peer, target):
        pltpu.make_async_copy(target, target, recv_sem.at[stage, mb, peer]).wait()

    def sent(stage, mb, source):
        def one(k, _):
            peer = lax.rem(me + k, narrows)
            pltpu.make_async_copy(source, source, send_sem.at[stage, mb, peer]).wait()
            return 0

        lax.fori_loop(1, narrows, one, 0)

    def part_rows(n):
        return pl.ds(pl.multiple_of(n * part, part), part)

    def to_all(body):
        def one(k, _):
            body(lax.rem(me + k, narrows))
            return 0

        lax.fori_loop(0, narrows, one, 0)

    def send_rows(which, mb):
        to_all(lambda peer: send(
            which, mb, uc.at[mb, which, part_rows(peer)], in_buf.at[mb, me, which], peer))

    for mb in range(micros):
        send_rows(CF, mb)
    for i in range(half):
        for j in range(wides):
            arrived(j, 2 * i + 1 - parity)
    own.wait()

    if rows == padded:
        pltpu.sync_copy(raw, wts)
    else:
        fold, group = padded // rows, raw.shape[1]
        for f in range(fold):
            start, stop = f * group, min((f + 1) * group, wts.shape[1])
            if start >= stop:
                break
            for i in range(width // LANES):
                here = lax.broadcasted_iota(jnp.int32, (LANES, raw.shape[0]), 0) + i * LANES
                there = lax.broadcasted_iota(jnp.int32, (LANES, raw.shape[0]), 1)
                match = (here // rows) * padded + f * rows + lax.rem(here, rows) == there
                take = jnp.where(match, 1.0, 0.0).astype(BF)
                wts[i * LANES : (i + 1) * LANES, start:stop] = dot(take, raw[:, : stop - start], 1, 0).astype(BF)
    extra = wts[:, 4 * width :]
    nrm[0:4, :] = norm_rows(extra, narrows)
    wc_buf[...] = jnp.where(lane < narrows, extra.astype(F32), 0).astype(BF)

    def forward(mb, hooks):
        def project(i, _):
            at = pl.ds(i * ROWS, ROWS)
            xhat, _ = norm_stats(pick(tok_ref, mb, at))
            al = (xhat * nrm[0:1, :] + nrm[1:2, :]).astype(BF)
            qkv_buf[mb, at, :] = dot(al, wq[...], 1, 0).astype(BF)
            return 0

        lax.fori_loop(0, blocks, project, 0)
        lse_col[...] = jnp.zeros_like(lse_col)
        keep = lax.broadcasted_iota(jnp.int32, (ROWS, ROWS), 1) <= lax.broadcasted_iota(jnp.int32, (ROWS, ROWS), 0)
        for i in range(blocks):
            keys = (i + 1) * ROWS
            at = pl.ds(i * ROWS, ROWS)

            def pair(hp, _, i=i, keys=keys, at=at):
                lanes = pl.ds(pl.multiple_of(hp * LANES, LANES), LANES)
                klanes = pl.ds(pl.multiple_of(hp * LANES + width, LANES), LANES)
                vlanes = pl.ds(pl.multiple_of(hp * LANES + 2 * width, LANES), LANES)
                q = qkv_buf[mb, at, lanes]
                k = qkv_buf[mb, pl.ds(0, keys), klanes]
                v = qkv_buf[mb, pl.ds(0, keys), vlanes]
                acc = None
                for h in range(2):
                    mine = lane // head == h
                    qm = jnp.where(mine, q * scale, 0).astype(BF)
                    vm = jnp.where(mine, v, 0).astype(BF)
                    s = dot(qm, k, 1, 1)
                    diag = jnp.where(keep, s[:, i * ROWS :], NEG_LARGE)
                    s = diag if i == 0 else jnp.concatenate([s[:, : i * ROWS], diag], axis=1)
                    m = jnp.max(s, axis=1, keepdims=True)
                    p = jnp.exp(s - m)
                    total = jnp.sum(p, axis=1, keepdims=True)
                    one = dot((p * (1.0 / total)).astype(BF), vm, 1, 0)
                    acc = one if acc is None else acc + one
                    lse_col[at, :] = jnp.where(lane == hp * 2 + h, m + jnp.log(total), lse_col[at, :])
                o_buf[mb, at, lanes] = acc.astype(BF)
                return 0

            lax.fori_loop(0, HEADS // 2, pair, 0)
            for hook in hooks.get(i, ()):
                hook()
        lse_buf[mb] = jnp.transpose(lse_col[...])[:HEADS, :]

        def finish(i, _):
            at = pl.ds(i * ROWS, ROWS)
            hidden = pick(tok_ref, mb, at) + dot(o_buf[mb, at, :], wo[...], 1, 0)
            xhat, _ = norm_stats(hidden)
            uc[mb, 0, at, :] = (xhat * nrm[2:3, :] + nrm[3:4, :]).astype(BF)
            return 0

        lax.fori_loop(0, blocks, finish, 0)

    def mix(mb):
        def logits(n, _):
            received(U, mb, n, in_buf.at[mb, n, 0])
            received(CF, mb, n, in_buf.at[mb, n, 1])
            w_buf[mb, n] = dot(in_buf[mb, n, 0], wc_buf[...], 1, 0).astype(BF).astype(F32)
            return 0

        lax.fori_loop(0, narrows, logits, 0)

        def rows_of(c, _):
            at = pl.ds(c * 16, 16)
            logit = [
                jnp.where(live_ref[mb, pl.ds(n, 1), :] > 0, w_buf[mb, n, at, :], NEG_LARGE) for n in range(narrows)
            ]
            top = functools.reduce(jnp.maximum, logit)
            exps = [jnp.exp(logit[n] - top) * live_ref[mb, pl.ds(n, 1), :] for n in range(narrows)]
            inverse = 1.0 / functools.reduce(jnp.add, exps)
            weights = [e * inverse for e in exps]
            for n in range(narrows):
                w_buf[mb, n, at, :] = weights[n]
            for which in range(2):
                values = [in_buf[mb, n, which, at, :].astype(F32) for n in range(narrows)]
                for e in range(narrows):
                    acc = functools.reduce(
                        jnp.add, [weights[n][:, e : e + 1] * values[n] for n in range(narrows)])
                    xd_out[mb, e, which, at, :] = acc.astype(BF)
            return 0

        lax.fori_loop(0, part // 16, rows_of, 0)
        to_all(lambda peer: send(XD, mb, xd_out.at[mb, peer], xd_in.at[mb, me], peer))

    def expert(mb):
        sent(U, mb, uc.at[mb, 0, pl.ds(0, part)])
        sent(CF, mb, uc.at[mb, 0, pl.ds(0, part)])

        def chunk(c, _):
            at = pl.ds(c * chunk_parts, chunk_parts)
            for k in range(chunk_parts):
                received(XD, mb, c * chunk_parts + k, xd_in.at[mb, c * chunk_parts + k])
            x = xd_in[mb, at, 0].reshape(ROWS, width)
            dy = xd_in[mb, at, 1].reshape(ROWS, width)

            def tile(j, carry):
                y, dx = carry
                cols = pl.ds(pl.multiple_of(j * width, width), width)
                z = dot(x, up_buf[:, cols], 1, 0)
                zz = z * z
                t = jnp.tanh(GELU_A * (z + GELU_B * z * zz))
                ga = (0.5 * z * (1.0 + t)).astype(BF)
                slope = 0.5 * (1.0 + t) + (0.5 * GELU_A) * z * (1.0 - t * t) * (1.0 + (3.0 * GELU_B) * zz)
                y = y + dot(ga, down_buf[cols, :], 1, 0)
                dz = (dot(dy, down_buf[cols, :], 1, 1) * slope).astype(BF)
                dx = dx + dot(dz, up_buf[:, cols], 1, 1)
                g_buf[folds + j] += dot(ga, dy, 0, 0)
                g_buf[j] += dot(x, dz, 0, 0)
                return y, dx

            zero = jnp.zeros((ROWS, width), F32)
            y, dx = lax.fori_loop(0, folds, tile, (zero, zero))
            xd_in[mb, at, 0] = y.astype(BF).reshape(chunk_parts, part, width)
            xd_in[mb, at, 1] = dx.astype(BF).reshape(chunk_parts, part, width)
            for k in range(chunk_parts):
                peer = c * chunk_parts + k
                send(YX, mb, xd_in.at[mb, peer], yx_in.at[mb, me], peer)
            return 0

        lax.fori_loop(0, blocks, chunk, 0)

    du_at = folds

    def du_rows(n):
        per = width // part
        return du_at + n // per, pl.ds(pl.multiple_of(lax.rem(n, per) * part, part), part)

    def combine(mb):
        sent(XD, mb, xd_out.at[mb, 0])

        def wait(e, _):
            received(YX, mb, e, yx_in.at[mb, e])
            return 0

        lax.fori_loop(0, narrows, wait, 0)

        def member(n, _):
            tile, rows_n = du_rows(n)

            def rows_of(c, _):
                at = pl.ds(c * 16, 16)
                u = in_buf[mb, n, 0, at, :].astype(F32)
                cf = in_buf[mb, n, 1, at, :].astype(F32)
                weights = w_buf[mb, n, at, :]
                mixed = du = None
                dw = jnp.zeros((16, LANES), F32)
                for e in range(narrows):
                    y = yx_in[mb, e, 0, at, :].astype(F32)
                    dx = yx_in[mb, e, 1, at, :].astype(F32)
                    weight = weights[:, e : e + 1]
                    mixed = weight * y if e == 0 else mixed + weight * y
                    du = weight * dx if e == 0 else du + weight * dx
                    dw = jnp.where(lane == e, jnp.sum(dx * u + cf * y, axis=1, keepdims=True), dw)
                xd_out[mb, n, 0, at, :] = mixed.astype(BF)
                g_buf[tile, pl.ds(pl.multiple_of(lax.rem(n, width // part) * part + c * 16, 16), 16), :] = du
                dw_buf[n, at, :] = dw
                return 0

            lax.fori_loop(0, part // 16, rows_of, 0)
            return 0

        lax.fori_loop(0, narrows, member, 0)

        def group(n, acc):
            return acc + w_buf[mb, n] * dw_buf[n]

        inner = lax.fori_loop(0, narrows, group, jnp.zeros((part, LANES), F32))

        def finish(n, _):
            tile, rows_n = du_rows(n)
            dc = (w_buf[mb, n] * (dw_buf[n] - inner)).astype(BF)
            du = g_buf[tile, rows_n, :] + dot(dc, wc_buf[...], 1, 1)
            xd_out[mb, n, 1] = du.astype(BF)
            dwc_ref[...] += dot(in_buf[mb, n, 0], dc, 0, 0)
            send(DU, mb, xd_out.at[mb, n, 1], uc.at[mb, 0, part_rows(me)], n)
            return 0

        lax.fori_loop(0, narrows, finish, 0)

    def send_mixed(mb):
        to_all(lambda peer: send(MIX, mb, xd_out.at[mb, peer, 0], uc.at[mb, 1, part_rows(me)], peer))

    tiles = length // width
    per_tile = width // ROWS

    def tile_rows(first, i):
        return first + i // per_tile, pl.ds(pl.multiple_of(lax.rem(i, per_tile) * ROWS, ROWS), ROWS)

    def out_copies(mb):
        copies = [pltpu.make_async_copy(o_buf.at[mb], out_ref.at[mb], io_sem.at[0])]
        for i in range(tiles):
            copies.append(pltpu.make_async_copy(
                g_buf.at[i], gt_ref.at[mb, pl.ds(i * width, width)], io_sem.at[1 + i]))
        return copies

    def backward(mb):
        to_all(lambda peer: received(DU, mb, peer, uc.at[mb, 0, part_rows(peer)]))

        def first(i, _):
            at = pl.ds(i * ROWS, ROWS)
            low = o_buf[mb, at, :]
            hidden = pick(tok_ref, mb, at) + dot(low, wo[...], 1, 0)
            tile, rows_i = tile_rows(tiles, i)
            g_buf[tile, rows_i, :] = hidden
            xhat, rstd = norm_stats(hidden)
            du = uc[mb, 0, at, :].astype(F32)
            dn[2:3, :] += jnp.sum(du * xhat, axis=0, keepdims=True)
            dn[3:4, :] += jnp.sum(du, axis=0, keepdims=True)
            dh = pick(cot_ref, mb, at) + norm_back(du, nrm[2:3, :], xhat, rstd)
            tile, rows_i = tile_rows(0, i)
            g_buf[tile, rows_i, :] = dh
            db = dh.astype(BF)
            dwo_ref[...] += dot(low, db, 0, 0)
            o_buf[mb, at, :] = dot(db, wo[...], 1, 1).astype(BF)
            return 0

        lax.fori_loop(0, blocks, first, 0)
        keep = lax.broadcasted_iota(jnp.int32, (ROWS, ROWS), 0) <= lax.broadcasted_iota(jnp.int32, (ROWS, ROWS), 1)

        def pair(hp, _):
            lanes = pl.ds(pl.multiple_of(hp * LANES, LANES), LANES)
            klanes = pl.ds(pl.multiple_of(hp * LANES + width, LANES), LANES)
            vlanes = pl.ds(pl.multiple_of(hp * LANES + 2 * width, LANES), LANES)
            for i in range(blocks):
                keys = (i + 1) * ROWS
                at = pl.ds(i * ROWS, ROWS)
                q = qkv_buf[mb, at, lanes]
                k = qkv_buf[mb, pl.ds(0, keys), klanes]
                v = qkv_buf[mb, pl.ds(0, keys), vlanes]
                do = o_buf[mb, at, lanes]
                dq = dk = dv = None
                for h in range(2):
                    mine = lane // head == h
                    qm = jnp.where(mine, q * scale, 0).astype(BF)
                    dom = jnp.where(mine, do, 0).astype(BF)
                    km = jnp.where(mine, k * scale, 0).astype(BF)
                    s = dot(k, qm, 1, 1) - lse_buf[mb, pl.ds(hp * 2 + h, 1), at]
                    diag = jnp.where(keep, s[i * ROWS :], NEG_LARGE)
                    p = jnp.exp(diag if i == 0 else jnp.concatenate([s[: i * ROWS], diag], axis=0))
                    pdp = p * dot(v, dom, 1, 1)
                    inner = jnp.sum(pdp, axis=0, keepdims=True)
                    ds = (pdp - p * inner).astype(BF)
                    a = dot(p.astype(BF), dom, 1, 0)
                    b = dot(ds, qm, 1, 0)
                    c = dot(ds, km, 0, 0)
                    dv, dk, dq = (a, b, c) if h == 0 else (dv + a, dk + b, dq + c)
                qkv_buf[mb, at, lanes] = dq.astype(BF)
                if i:
                    dk_ref[: i * ROWS, :] += dk[: i * ROWS]
                    dv_ref[: i * ROWS, :] += dv[: i * ROWS]
                dk_ref[i * ROWS : keys, :] = dk[i * ROWS :]
                dv_ref[i * ROWS : keys, :] = dv[i * ROWS :]
            qkv_buf[mb, :, klanes] = dk_ref[...].astype(BF)
            qkv_buf[mb, :, vlanes] = dv_ref[...].astype(BF)
            return 0

        lax.fori_loop(0, HEADS // 2, pair, 0)
        to_all(lambda peer: received(MIX, mb, peer, uc.at[mb, 1, part_rows(peer)]))

        def last(i, _):
            at = pl.ds(i * ROWS, ROWS)
            xhat, rstd = norm_stats(pick(tok_ref, mb, at))
            al = (xhat * nrm[0:1, :] + nrm[1:2, :]).astype(BF)
            dqkv = qkv_buf[mb, at, :]
            dwq_ref[...] += dot(al, dqkv, 0, 0)
            da = dot(dqkv, wq[...], 1, 1)
            dn[0:1, :] += jnp.sum(da * xhat, axis=0, keepdims=True)
            dn[1:2, :] += jnp.sum(da, axis=0, keepdims=True)
            tile, rows_i = tile_rows(0, i)
            g_buf[tile, rows_i, :] = g_buf[tile, rows_i, :] + norm_back(da, nrm[0:1, :], xhat, rstd)
            tile, rows_i = tile_rows(tiles, i)
            o_buf[mb, at, :] = (g_buf[tile, rows_i, :] + uc[mb, 1, at, :].astype(F32)).astype(BF)
            return 0

        lax.fori_loop(0, blocks, last, 0)
        for copy in out_copies(mb):
            copy.start()

    def relay(hop):
        def run():
            hop_arrived(hop)
            if hop < wides - 1:
                hop_send(hop + 1)

        return run

    relays = [relay(hop) for hop in range(1, wides - 1)]
    for mb in range(micros):
        hooks = {}
        if mb == 0 and relays:
            hooks[min(2, blocks - 1)] = [relays.pop(0)]
        elif relays and mb == micros - 1:
            hooks[min(1, blocks - 1)] = relays
        if mb > 0:
            hooks[min(2, blocks - 1)] = [functools.partial(mix, mb - 1)]
        forward(mb, hooks)
        send_rows(U, mb)
    mix(micros - 1)
    hop_arrived(wides - 1)
    g_buf[...] = jnp.zeros_like(g_buf)
    for mb in range(micros):
        expert(mb)
    for hop in range(1, wides):
        hop_sent(hop)

    for j in range(folds):
        up_buf[:, j * width : (j + 1) * width] = g_buf[j].astype(BF)
        down_buf[j * width : (j + 1) * width, :] = g_buf[folds + j].astype(BF)
    for k, z in enumerate(z_peers):
        remote(up_part(z), gotup_ref.at[k], rs_sem.at[k, 0], rsr_sem.at[k, 0], (z, me)).start()
        remote(down_part(z), gotdown_ref.at[k], rs_sem.at[k, 1], rsr_sem.at[k, 1], (z, me)).start()
    owned = [
        pltpu.make_async_copy(
            g_buf.at[j, pl.ds(pl.multiple_of(w_id * up_rows, up_rows), up_rows)],
            ownup_ref.at[:, pl.ds(j * width, width)], own_sem.at[1 + j])
        for j in range(folds)
    ]
    piece = min(down_rows, width)
    first_row = w_id * down_rows
    for j in range(down_rows // piece):
        row = first_row + j * piece
        owned.append(pltpu.make_async_copy(
            g_buf.at[folds + row // width, pl.ds(pl.multiple_of(lax.rem(row, width), piece), piece)],
            owndown_ref.at[pl.ds(j * piece, piece)], own_sem.at[1 + folds + j]))
    for copy in owned:
        copy.start()
    for copy in owned:
        copy.wait()

    dwq_ref[...] = jnp.zeros_like(dwq_ref)
    dwo_ref[...] = jnp.zeros_like(dwo_ref)
    dn[...] = jnp.zeros_like(dn)
    for mb in range(micros):
        combine(mb)
    for mb in range(micros):
        send_mixed(mb)
    for mb in range(micros):
        if mb > 0:
            for copy in out_copies(mb - 1):
                copy.wait()
        backward(mb)
    dex_ref[...] = jnp.transpose(jnp.concatenate([dn[...], jnp.zeros((LANES - 8, width), F32)], axis=0))

    for copy in out_copies(micros - 1):
        copy.wait()
    for copy in gather_sends:
        copy.wait_send()
    for k in range(wides - 1):
        for i, (mine, theirs) in enumerate(((up_part(0), gotup_ref.at[k]), (down_part(0), gotdown_ref.at[k]))):
            pltpu.make_async_copy(mine, mine, rs_sem.at[k, i]).wait()
            pltpu.make_async_copy(theirs, theirs, rsr_sem.at[k, i]).wait()
    for mb in range(micros):
        sent(YX, mb, xd_in.at[mb, 0])
        sent(DU, mb, xd_out.at[mb, 0, 0])
        sent(MIX, mb, xd_out.at[mb, 0, 0])


def run_block(flags, live, tokens, cot, shard, up, down, wides, narrows, rows):
    micros, length, width = tokens.shape
    part = length // narrows
    hidden_width = up.shape[1]
    folds = hidden_width // width
    devices = wides * narrows
    hbm = pl.BlockSpec(memory_space=pl.ANY)
    vmem = pl.BlockSpec(memory_space=pltpu.VMEM)
    pairs = pltpu.VMEM((micros, narrows, 2, part, width), BF)
    sems = pltpu.SemaphoreType.DMA
    half = narrows // 2
    cols = 4 * width + LANES
    return pl.pallas_call(
        functools.partial(block_kernel, wides, narrows, rows),
        out_shape=[
            jax.ShapeDtypeStruct((micros, length, width), F32),
            jax.ShapeDtypeStruct((micros, length, width), BF),
            jax.ShapeDtypeStruct((width, 3 * width), F32),
            jax.ShapeDtypeStruct((width, width), F32),
            jax.ShapeDtypeStruct((width, LANES), F32),
            jax.ShapeDtypeStruct((width, LANES), F32),
            jax.ShapeDtypeStruct(up.shape, F32),
            jax.ShapeDtypeStruct(down.shape, F32),
            jax.ShapeDtypeStruct((wides - 1,) + up.shape, BF),
            jax.ShapeDtypeStruct((wides - 1,) + down.shape, BF),
        ],
        in_specs=[vmem] * 7,
        out_specs=[hbm, hbm, vmem, vmem, vmem, vmem, hbm, hbm, hbm, hbm],
        scratch_shapes=[
            pltpu.VMEM((devices * shard.shape[0], shard.shape[1]), BF),
            pltpu.VMEM((width, cols), BF),
            pltpu.VMEM((micros, 2, length, width), BF),
            pltpu.VMEM((micros, length, 3 * width), BF),
            pltpu.VMEM((micros, length, width), BF),
            pltpu.VMEM((micros, HEADS, length), F32),
            pltpu.VMEM((length, LANES), F32),
            pltpu.VMEM((8, width), F32),
            pltpu.VMEM((8, width), F32),
            pairs,
            pairs,
            pairs,
            pairs,
            pltpu.VMEM((micros, narrows, part, LANES), F32),
            pltpu.VMEM((narrows, part, LANES), F32),
            pltpu.VMEM((width, LANES), BF),
            pltpu.VMEM((width, hidden_width), BF),
            pltpu.VMEM((hidden_width, width), BF),
            pltpu.VMEM((2 * folds, width, width), F32),
            pltpu.VMEM((length, LANES), F32),
            pltpu.VMEM((length, LANES), F32),
            sems((wides - 1,)),
            sems((wides, half - 1)),
            sems((wides, half)),
            sems((wides, narrows)),
            sems((wides - 1, 2, 2)),
            sems((wides - 1, 2, 2)),
            sems((6, micros, narrows)),
            sems((6, micros, narrows)),
            sems((wides - 1, 2)),
            sems((wides - 1, 2)),
            sems((1 + 2 * folds,)),
            sems((1 + length // width,)),
        ],
        compiler_params=pltpu.CompilerParams(
            collective_id=0, has_side_effects=True, vmem_limit_bytes=64 << 20),
        name="block",
    )(flags, live, tokens, cot, shard, up, down)


def reduce_kernel(wides, narrows, wq_ref, wo_ref, ex_ref, dwc_ref, out_ref,
                  s1, r1, s2, r2, s3, r3, total, c_sem, p_sem, z_sem, cr_sem, pr_sem, zr_sem):
    w, n = lax.axis_index("wide"), lax.axis_index("narrow")
    half = narrows // 2
    q, parity = n // 2, lax.rem(n, 2)
    core = n + 1 - 2 * parity
    z_peers = [lax.rem(w + k, wides) for k in range(1, wides)]
    p_peers = [lax.rem(q + k, half) for k in range(1, half)]
    greet([(w, core)] + [(w, p * 2 + parity) for p in p_peers] + [(z, n) for z in z_peers])
    a, b = wq_ref.shape[2], wq_ref.shape[2] + wo_ref.shape[2]

    def parts(index):
        return wq_ref[index], wo_ref[index], ex_ref[index] + dwc_ref[index]

    sends = []
    for k in range(half):
        there = lax.rem(q + 1 + k, half)

        def fill(z, _, there=there):
            one, two, three = parts(z * narrows + 2 * there + 1 - parity)
            s1[there, z, :, :a] = one.astype(BF)
            s1[there, z, :, a:b] = two.astype(BF)
            s1[there, z, :, b:] = three.astype(BF)
            return 0

        lax.fori_loop(0, wides, fill, 0)
        copy = remote(s1.at[there], r1.at[there], c_sem.at[k], cr_sem.at[there], (w, core))
        copy.start()
        sends.append(copy)
    for k in range(half):
        there = lax.rem(q + 1 + k, half)
        remote(s1.at[there], r1.at[there], c_sem.at[k], cr_sem.at[there], (w, core)).wait_recv()
        last = k == half - 1

        def add(z, _, there=there, last=last):
            one, two, three = parts(z * narrows + 2 * there + parity)
            got = r1[there, z].astype(F32)
            one, two, three = one + got[:, :a], two + got[:, a:b], three + got[:, b:]
            if last:
                total[z, :, :a], total[z, :, a:b], total[z, :, b:] = one, two, three
            else:
                s2[there, z, :, :a] = one.astype(BF)
                s2[there, z, :, a:b] = two.astype(BF)
                s2[there, z, :, b:] = three.astype(BF)
            return 0

        lax.fori_loop(0, wides, add, 0)
        if not last:
            copy = remote(s2.at[there], r2.at[q], p_sem.at[k], pr_sem.at[q], (w, there * 2 + parity))
            copy.start()
            sends.append(copy)
    for k in range(1, half):
        there = lax.rem(q + k, half)
        remote(s2.at[there], r2.at[there], p_sem.at[0], pr_sem.at[there], (w, n)).wait_recv()
    for k in range(wides):
        z = lax.rem(w + 1 + k, wides)
        acc = total[z]
        for i in range(1, half):
            acc = acc + r2[lax.rem(q + i, half), z].astype(F32)
        if k < wides - 1:
            s3[z] = acc.astype(BF)
            copy = remote(s3.at[z], r3.at[w], z_sem.at[k], zr_sem.at[w], (z, n))
            copy.start()
            sends.append(copy)
        else:
            out_ref[...] = acc
    for k in range(1, wides):
        z = lax.rem(w + k, wides)
        remote(s3.at[z], r3.at[z], z_sem.at[0], zr_sem.at[z], (w, n)).wait_recv()
        out_ref[...] += r3[z].astype(F32)
    for copy in sends:
        copy.wait_send()


def reduce_shared(dwq, dwo, dex, dwc, wides, narrows):
    half = narrows // 2
    rows = dwq.shape[1]
    cols = dwq.shape[2] + dwo.shape[2] + dex.shape[2]
    vmem = pl.BlockSpec(memory_space=pltpu.VMEM)
    block = (half, wides, rows, cols)
    sems = pltpu.SemaphoreType.DMA
    return pl.pallas_call(
        functools.partial(reduce_kernel, wides, narrows),
        out_shape=jax.ShapeDtypeStruct((rows, cols), F32),
        in_specs=[vmem] * 4,
        out_specs=vmem,
        scratch_shapes=[pltpu.VMEM(block, BF)] * 4
        + [pltpu.VMEM(block[1:], BF)] * 2
        + [pltpu.VMEM(block[1:], F32)]
        + [sems((half,)), sems((half,)), sems((wides,))] * 2,
        compiler_params=pltpu.CompilerParams(
            collective_id=2, has_side_effects=True, vmem_limit_bytes=60 << 20),
        name="reduce_shared",
    )(dwq, dwo, dex, dwc)


def total_kernel(wides, narrows, part_ref, out_ref, got_n, mid, got_w, send_n, recv_n, send_w, recv_w):
    w, n = lax.axis_index("wide"), lax.axis_index("narrow")
    n_peers = [lax.rem(n + k, narrows) for k in range(1, narrows)]
    z_peers = [lax.rem(w + k, wides) for k in range(1, wides)]
    greet([(w, p) for p in n_peers] + [(z, n) for z in z_peers])
    sends = []
    for k, p in enumerate(n_peers):
        copy = remote(part_ref, got_n.at[n], send_n.at[k], recv_n.at[n], (w, p))
        copy.start()
        sends.append(copy)
    got_n[n] = part_ref[...]
    for p in n_peers:
        remote(part_ref, got_n.at[p], send_n.at[0], recv_n.at[p], (w, n)).wait_recv()
    acc = got_n[0]
    for k in range(1, narrows):
        acc = acc + got_n[k]
    mid[...] = acc
    got_w[w] = acc
    for k, z in enumerate(z_peers):
        copy = remote(mid, got_w.at[w], send_w.at[k], recv_w.at[w], (z, n))
        copy.start()
        sends.append(copy)
    for z in z_peers:
        remote(mid, got_w.at[z], send_w.at[0], recv_w.at[z], (w, n)).wait_recv()
    acc = got_w[0]
    for k in range(1, wides):
        acc = acc + got_w[k]
    out_ref[...] = acc
    for copy in sends:
        copy.wait_send()


def sum_everywhere(part, wides, narrows):
    vmem = pl.BlockSpec(memory_space=pltpu.VMEM)
    sems = pltpu.SemaphoreType.DMA
    return pl.pallas_call(
        functools.partial(total_kernel, wides, narrows),
        out_shape=jax.ShapeDtypeStruct(part.shape, F32),
        in_specs=[vmem],
        out_specs=vmem,
        scratch_shapes=[
            pltpu.VMEM((narrows,) + part.shape, F32),
            pltpu.VMEM(part.shape, F32),
            pltpu.VMEM((wides,) + part.shape, F32),
            sems((narrows - 1,)),
            sems((narrows,)),
            sems((wides - 1,)),
            sems((wides,)),
        ],
        compiler_params=pltpu.CompilerParams(collective_id=3, has_side_effects=True),
        name="sum_everywhere",
    )(part)


def adam_update(weight, first_state, second_state, gradient, factor, rate, decay):
    clipped = gradient * factor
    first_new = BETA_ONE * first_state + (1.0 - BETA_ONE) * clipped
    second_new = BETA_TWO * second_state + (1.0 - BETA_TWO) * clipped * clipped
    first_hat = first_new / (1.0 - BETA_ONE**STEP)
    second_hat = second_new / (1.0 - BETA_TWO**STEP)
    weight_new = weight - rate * (first_hat / (jnp.sqrt(second_hat) + ADAM_EPS) + decay * weight)
    return (weight_new, first_new, second_new, weight_new.astype(BF))


def per_device(
    tokens, cotangent, seq_counts, micro_assign,
    norm_params, norm_first, norm_second,
    project_weight, project_first, project_second,
    output_weight, output_first, output_second,
    control_weight, control_first, control_second,
    up_weight, up_first, up_second,
    down_weight, down_first, down_second,
):
    wides, narrows = lax.axis_size("wide"), lax.axis_size("narrow")
    wide_index, narrow_index = lax.axis_index("wide"), lax.axis_index("narrow")
    devices = wides * narrows
    micro_count, length, width = tokens.shape
    experts = control_weight.shape[1]
    rows = project_weight.shape[0]
    padded = max(rows, 16)

    first_device = wide_index * narrows
    row_counts = lax.dynamic_slice_in_dim(seq_counts, first_device, narrows)
    row_assign = lax.dynamic_slice_in_dim(micro_assign, first_device, narrows, 0)
    slot_numbers = jnp.arange(micro_count, dtype=jnp.int32)
    micros = jnp.arange(micro_count, dtype=jnp.int32)
    member_slots = jnp.sum(
        slot_numbers[None, None, :] * (row_assign[None] == micros[:, None, None]).astype(jnp.int32), axis=2
    )
    live = (member_slots < row_counts[None]).astype(F32)
    live = jnp.broadcast_to(live[:, :, None], (micro_count, narrows, LANES))
    slots = lax.dynamic_index_in_dim(member_slots, narrow_index, 1, keepdims=False)
    flags = (slots[:, None] == slot_numbers[None, :]).astype(F32).reshape(-1, 1)
    flags = jnp.pad(jnp.broadcast_to(flags, (flags.shape[0], LANES)), ((0, -flags.shape[0] % 8), (0, 0)))

    norm_turned = norm_params.T
    high = lax.reduce_precision(norm_turned, 8, 7)
    middle = lax.reduce_precision(norm_turned - high, 8, 7)
    lower = norm_turned - high - middle
    extra = jnp.concatenate([control_weight, high, middle, lower], axis=1).astype(BF)
    extra = jnp.pad(extra, ((0, 0), (0, LANES - extra.shape[1])))
    shard = jnp.concatenate([project_weight.astype(BF), output_weight.astype(BF), extra], axis=1)
    if rows < padded:
        fold = padded // rows
        group = -(-(shard.shape[1] // LANES) // fold) * LANES
        shard = jnp.pad(shard, ((0, 0), (0, fold * group - shard.shape[1])))
        shard = shard.reshape(rows, fold, group).transpose(1, 0, 2).reshape(padded, group)

    grad_rows, out_low, dwq, dwo, dex, dwc, own_up, own_down, got_up, got_down = run_block(
        flags, live, tokens, cotangent, shard, up_weight[0], down_weight[0], wides, narrows, rows)
    place = [micro_assign[first_device + narrow_index, j] for j in range(micro_count)]
    grad_tokens = jnp.stack([lax.dynamic_index_in_dim(grad_rows, place[j], 0, False) for j in range(micro_count)])
    out_rows = jnp.stack([lax.dynamic_index_in_dim(out_low, place[j], 0, False) for j in range(micro_count)])
    up_grad = own_up + jnp.sum(got_up.astype(F32), axis=0)
    down_grad = own_down + jnp.sum(got_down.astype(F32), axis=0)
    dex = jnp.pad(dex[:, :4], ((0, 0), (experts, LANES - 4 - experts)))

    def by_owner(grad):
        return jnp.pad(grad.reshape(devices, rows, -1), ((0, 0), (0, padded - rows), (0, 0)))

    shared = reduce_shared(by_owner(dwq), by_owner(dwo), by_owner(dex), by_owner(dwc), wides, narrows)[:rows]
    project_grad = shared[:, : 3 * width]
    output_grad = shared[:, 3 * width : 4 * width]
    control_grad = shared[:, 4 * width : 4 * width + experts]
    norm_grad = shared[:, 4 * width + experts : 4 * width + experts + 4].T
    squares = jnp.sum(shared * shared) + jnp.sum(up_grad * up_grad) + jnp.sum(down_grad * down_grad)
    total = sum_everywhere(jnp.full((8, LANES), squares, F32), wides, narrows)
    grad_norm = jnp.sqrt(total[0, 0])
    factor = CLIP_NORM / jnp.maximum(grad_norm, CLIP_NORM)
    norm_out = adam_update(norm_params, norm_first, norm_second, norm_grad, factor, 0.3, 0.0)
    project_out = adam_update(
        project_weight, project_first, project_second, project_grad, factor, 0.03, DECAY_RATE)
    output_out = adam_update(output_weight, output_first, output_second, output_grad, factor, 0.2, DECAY_RATE)
    control_out = adam_update(
        control_weight, control_first, control_second, control_grad, factor, 0.015, DECAY_RATE)
    up_out = adam_update(up_weight, up_first, up_second, up_grad[None], factor, 0.1, DECAY_RATE)
    down_out = adam_update(down_weight, down_first, down_second, down_grad[None], factor, 0.1, DECAY_RATE)
    return (out_rows, grad_tokens, grad_norm) + norm_out + project_out + output_out + control_out + up_out + down_out


def solution(mesh):
    both = ("wide", "narrow")
    rows3, cols, rows2, expert = P(both, None, None), P(None, both), P(both, None), P("narrow", "wide", None)
    return jax.shard_map(
        per_device,
        mesh=mesh,
        in_specs=(rows3, rows3, P(), P()) + (cols,) * 3 + (rows2,) * 9 + (expert,) * 6,
        out_specs=(rows3, rows3, P()) + (cols,) * 4 + (rows2,) * 12 + (expert,) * 8,
        check_vma=False,
    )
```

time: 432 us -> 358 us (0.83)
  Pallas kernels: 364 us -> 312 us
  between operations: 21.5 us -> 8.67 us
  waiting for transfers between devices: 6.59 us -> 0 us
  other arithmetic: 24.6 us -> 19.3 us
    pallas_call x4 -> x1, Pallas kernels: 322 us -> 265 us  [run_block(): pl.pallas_call(functools.partial(block_kernel, wides, narrows, rows), out...]
    all_gather x1 -> x0, waiting for transfers between devices: 6.56 us -> none  [per_device(): upd = lax.all_gather(packed, 'wide', axis=0, tiled=False)]
    pallas_call x1, Pallas kernels: 29.4 us -> 35.6 us  [reduce_shared(): pl.pallas_call(functools.partial(reduce_kernel, wides, narrows), out_shap...]
  transfers between devices with their start and end apart: 2 -> 0, of which waited for: 1 -> 0; matrix products, arithmetic and copies ran while one was open for 3% -> 0% of each run, Pallas kernels for 38% -> 0%
where the time goes in v2:
time: 358 us
  Pallas kernels  312 us (87%)
  other arithmetic  19.3 us (5%)
  local copies, waits for them, and re-layouts  17.6 us (5%)
  between operations  8.67 us (2%)
    pallas_call x1, Pallas kernels, run_block(): pl.pallas_call(functools.partial(block_kernel, wides, narrows, rows), out...  265 us
    pallas_call x1, Pallas kernels, reduce_shared(): pl.pallas_call(functools.partial(reduce_kernel, wides, narrows), out_shap...  35.6 us
    pallas_call x1, Pallas kernels, sum_everywhere(): pl.pallas_call(functools.partial(total_kernel, wides, narrows), out_shape...  11.2 us
    convert_element_type x6, other arithmetic, adam_update(): return (weight_new, first_new, second_new, weight_new.astype(BF))  8.15 us
    unnamed x62, local copies, waits for them, and re-layouts  7.45 us

profile of v2, /device:TPU:0, one launch (start us, length us, event | category | flops | bytes accessed | tf_op | source)
XLA Modules:
  0.0 357.9 jit_solution(5386878602988594406)
XLA Ops:
  0.7 0.8 constant_dynamic-slice_fusion.6
  1.4 0.7 dynamic_slice.32
  2.2 0.7 broadcast_in_dim.4.live_ref
  3.2 0.7 pad.18.flag_ref
  3.9 0.8 copy.105
  4.6 0.7 convert.15
  5.5 0.9 convert_element_type.55
  6.4 0.8 convert_element_type.56
  7.8 265.5 %block.1 = (f32[2,1024,512]{2,1,0:T(8,128)}, bf16[2,1024,512]{2,1,0:T(8,128)(2,1)}, f32[512,1536]{1,0:T(8,128)}, f32[512,512]{1,0:T(8,128)}, f32[512,128]{1,0:T(...) custom-call(f32[8,128]{1,0:T(8,128)} %pad.18.flag_ref, ...), custom_call_target="tpu_custom_call" | custom-call | tf_op jit(solution)/shard_map/block/pallas_call | solution.py:620
  273.3 1.8 pad.20
  275.1 35.6 %reduce_shared.1 = f32[16,2176]{1,0:T(8,128)} custom-call(f32[32,16,1536]{2,1,0:T(8,128)} %bitcast.44, f32[32,16,512]{2,1,0:T(8,128)} %bitcast.45, f32[32,16,128]{2,1,0:T(8,128)} %bitcast.46, f32[32,16,128]{2,1,0:T(8,128)} %bitcast.47), custom_call_target="tpu_custom_call" | custom-call | tf_op jit(solution)/shard_map/reduce_shared/pallas_call | solution.py:758
  310.7 1.6 multiply_reduce_fusion.2
  312.7 0.9 multiply_reduce_fusion.1
  315.1 0.9 copy-done.8
  316.1 0.9 multiply_reduce_fusion
  318.3 11.2 %sum_everywhere.1 = f32[8,128]{1,0:T(8,128)} custom-call(f32[8,128]{1,0:T(8,128)} %broadcast_in_dim.5.part_ref), custom_call_target="tpu_custom_call" | custom-call | tf_op jit(solution)/shard_map/sum_everywhere/pallas_call | solution.py:808
  329.5 1.2 slice.19
  331.5 4.1 %fusion.20 = (bf16[1,512,512]{2,1,0:T(8,128)(2,1)}, f32[1,512,512]{2,1,0:T(8,128)}, f32[1,512,512]{2,1,0:T(8,128)}, f32[1,512,512]{2,1,0:T(8,128)}) fusion(f32[1,512,512]{2,1,0:T(8,128)S(1)} %copy-done, f32[512,512]{1,0:T(8,128)S(1)} %get-tuple-element.180, f32[]{:T(128)S(6)} %div.57, f32[1,512,512]{2,1,0:T(8,128)} %param.42, f32[1,512,512]{2,1,0:T(8,128)} %param.43), kind=kLoop, calls=%fused_computation.67 | loop fusion | flops 4194304 | bytes 7864324 | tf_op jit(solution)/shard_map/convert_element_type | solution.py:834
  335.8 2.5 fusion.23
  338.5 0.7 copy.125
  341.9 0.8 fusion.30
  350.0 2.7 constant_dynamic-slice_fusion.1
  352.7 2.5 pad_maximum_fusion
  355.3 1.5 pad_maximum_fusion.1
  (77 shorter events, 8.9 us)
Async XLA Ops:
  4.6 3.2 copy-start.14
  275.1 37.3 %copy-start.4 = (bf16[3,128,2048]{2,1,0:T(8,128)(2,1)S(1)}, bf16[3,128,2048]{2,1,0:T(8,128)(2,1)}, u32[]{:S(2)}) copy-start(bf16[3,128,2048]{2,1,0:T(8,128)(2,1)} %get-tuple-element.44) | copy-start | bytes 4718596
  310.7 1.9 copy-start.9
  312.7 2.2 copy-start.3
  314.9 1.2 copy-start.8
  315.1 16.3 %copy-start = (f32[1,512,512]{2,1,0:T(8,128)S(1)}, f32[1,512,512]{2,1,0:T(8,128)}, u32[]{:S(2)}) copy-start(f32[1,512,512]{2,1,0:T(8,128)} %param.41) | copy-start | bytes 3145732
  331.5 4.2 %copy-start.1 = (f32[1,128,2048]{2,1,0:T(8,128)S(1)}, f32[1,128,2048]{2,1,0:T(8,128)}, u32[]{:S(2)}) copy-start(f32[1,128,2048]{2,1,0:T(8,128)} %param.38) | copy-start | bytes 3145732
  331.5 4.2 %copy-start.6 = (f32[1,128,2048]{2,1,0:T(8,128)S(1)}, f32[1,128,2048]{2,1,0:T(8,128)}, u32[]{:S(2)}) copy-start(f32[1,128,2048]{2,1,0:T(8,128)} %param.39) | copy-start | bytes 3145732
  331.5 4.2 %copy-start.7 = (f32[1,128,2048]{2,1,0:T(8,128)S(1)}, f32[1,128,2048]{2,1,0:T(8,128)}, u32[]{:S(2)}) copy-start(f32[1,128,2048]{2,1,0:T(8,128)} %param.40) | copy-start | bytes 3145732
  335.7 2.6 copy-start.19
  335.7 2.7 copy-start.20
  335.7 2.8 copy-start.18
  335.7 2.8 copy-start.5
  335.7 5.5 %copy-start.11 = (f32[16,512]{1,0:T(8,128)S(1)}, f32[16,512]{1,0:T(8,128)}, u32[]{:S(2)}) copy-start(f32[16,512]{1,0:T(8,128)} %param.32) | copy-start | bytes 98308
  335.7 5.5 %copy-start.16 = (f32[16,512]{1,0:T(8,128)S(1)}, f32[16,512]{1,0:T(8,128)}, u32[]{:S(2)}) copy-start(f32[16,512]{1,0:T(8,128)} %param.33) | copy-start | bytes 98308
  335.7 5.5 %copy-start.17 = (f32[16,512]{1,0:T(8,128)S(1)}, f32[16,512]{1,0:T(8,128)}, u32[]{:S(2)}) copy-start(f32[16,512]{1,0:T(8,128)} %param.34) | copy-start | bytes 98308
  335.7 6.1 %copy-start.10 = (f32[16,1536]{1,0:T(8,128)S(1)}, f32[16,1536]{1,0:T(8,128)}, u32[]{:S(2)}) copy-start(f32[16,1536]{1,0:T(8,128)} %param.29) | copy-start | bytes 294916
  335.7 6.1 %copy-start.12 = (f32[16,1536]{1,0:T(8,128)S(1)}, f32[16,1536]{1,0:T(8,128)}, u32[]{:S(2)}) copy-start(f32[16,1536]{1,0:T(8,128)} %param.30) | copy-start | bytes 294916
  335.8 6.1 %copy-start.13 = (f32[16,1536]{1,0:T(8,128)S(1)}, f32[16,1536]{1,0:T(8,128)}, u32[]{:S(2)}) copy-start(f32[16,1536]{1,0:T(8,128)} %param.31) | copy-start | bytes 294916
  335.8 6.9 %copy-start.22 = (f32[4,16]{1,0:T(4,128)S(1)}, f32[4,16]{1,0:T(4,128)}, u32[]{:S(2)}) copy-start(f32[4,16]{1,0:T(4,128)} %param.27) | copy-start | bytes 772
  335.8 6.9 %copy-start.23 = (f32[4,16]{1,0:T(4,128)S(1)}, f32[4,16]{1,0:T(4,128)}, u32[]{:S(2)}) copy-start(f32[4,16]{1,0:T(4,128)} %param.28) | copy-start | bytes 772
  335.8 7.0 %copy-start.15 = (f32[4,16]{0,1:T(8,128)S(1)}, f32[4,16]{0,1:T(8,128)}, u32[]{:S(2)}) copy-start(f32[4,16]{0,1:T(8,128)} %copy-done.14) | copy-start | bytes 772
  335.8 9.7 %copy-start.21 = (s32[32,2]{0,1:T(2,128)S(1)}, s32[32,2]{0,1:T(2,128)}, u32[]{:S(2)}) copy-start(s32[32,2]{0,1:T(2,128)} %param.25) | copy-start | bytes 772
  352.7 2.5 copy-start.2
